TPU v7x, 512 devices: a whole 4x4x16 slice. The times are simulated.
512 devices in a mesh: ckpt: 2 (over x_hi), ex: 8 (over y, x_lo), par: 32 (over z, core).
Axes of the slice: x: 4 (x_hi: 2, x_lo: 2; x = x_hi * 2 + x_lo), y: 4, z: 16, core: 2. Of those that a mesh axis runs over, the one named last changes fastest.
Arguments:
- example_token_inputs: bfloat16 [2, 192, 128, 8192], P('ckpt', 'ex', None, 'par'), may hold values from -6 to 6
- example_token_cotangents: bfloat16 [2, 192, 128, 8192], P('ckpt', 'ex', None, 'par'), may hold values from -6 to 6
- query_token_inputs: bfloat16 [2, 64, 128, 8192], P('ckpt', 'ex', None, 'par'), may hold values from -6 to 6
- query_token_cotangents: bfloat16 [2, 64, 128, 8192], P('ckpt', 'ex', None, 'par'), may hold values from -6 to 6
- example_token_lengths: int32 [192], P('ex'), may hold values from 16 to 128
- query_token_lengths: int32 [64], P('ex'), may hold values from 16 to 128
- adapter_down_snapshots: bfloat16 [2, 8192, 64], P('ckpt', 'par'), may hold values from -0.25 to 0.25
- adapter_up_snapshots: bfloat16 [2, 64, 8192], P('ckpt', None, 'par'), may hold values from -0.1875 to 0.1875
- down_first_moment: float32 [2, 8192, 64], P('ckpt', 'par'), may hold values from -0.3 to 0.3
- down_second_moment: float32 [2, 8192, 64], P('ckpt', 'par'), may hold values from 0.001 to 0.16
- up_first_moment: float32 [2, 64, 8192], P('ckpt', None, 'par'), may hold values from -0.3 to 0.3
- up_second_moment: float32 [2, 64, 8192], P('ckpt', None, 'par'), may hold values from 0.001 to 0.16
- snapshot_learning_rates: float32 [2], P('ckpt'), may hold values from 0.5 to 4
Outputs:
- scores: float32 [192, 64], P('ex')
All inputs are finite; a program needn't handle non-finite values.
Results may differ from a plain program's by a relative error of at most 0.0003.
Values may be sent and summed in bfloat16 or wider, within the bound.
A program may use at most 64 MiB of HBM per device.

v0:
```python
import jax
import jax.numpy as jnp
from jax import lax
from jax.sharding import PartitionSpec as P

ADAM_ONE = 0.9
ADAM_TWO = 0.999
ADAM_EPS = 1e-08
NORM_EPS = 1e-06


def local_projections(inputs, cotangents, adapter_down_weight, adapter_up_weight):
    examples, slots, features = inputs.shape
    flat_inputs = inputs.reshape(examples * slots, features)
    flat_back = cotangents.reshape(examples * slots, cotangents.shape[2])
    hidden_proj = jnp.dot(flat_inputs, adapter_down_weight, preferred_element_type=jnp.float32)
    back_proj = lax.dot_general(
        flat_back, adapter_up_weight, (((1,), (1,)), ((), ())), preferred_element_type=jnp.float32
    )
    return jnp.concatenate([hidden_proj, back_proj], axis=1)


def weigh(combined, lengths, slots):
    row_count = combined.shape[0]
    row_index = jnp.arange(row_count, dtype=jnp.int32)
    position = row_index % slots
    owner = row_index // slots
    picked = owner[:, None] == jnp.arange(lengths.shape[0], dtype=jnp.int32)[None, :]
    length = jnp.sum(jnp.where(picked, lengths[None, :], 0), axis=1)
    weight = jnp.where(position < length, 1.0 / length.astype(jnp.float32), jnp.float32(0.0))
    return (combined * weight[:, None]).astype(jnp.bfloat16)


def example_gradients(inputs, cotangents, weighted_flat):
    examples, slots, features = inputs.shape
    ranks = weighted_flat.shape[1] // 2
    weighted = weighted_flat.reshape(examples, slots, 2 * ranks)
    hidden_w = weighted[:, :, :ranks]
    back_w = weighted[:, :, ranks:]
    grad_up = jnp.einsum("etr,eto->ero", hidden_w, cotangents, preferred_element_type=jnp.float32)
    grad_down = jnp.einsum("etd,etr->edr", inputs, back_w, preferred_element_type=jnp.float32)
    return jnp.concatenate([grad_down.reshape(examples, -1), grad_up.reshape(examples, -1)], axis=1)


def normalized(products, demo_norms, query_norms, learning):
    return (
        learning
        * products
        * lax.rsqrt(demo_norms + NORM_EPS)[:, None]
        * lax.rsqrt(query_norms + NORM_EPS)[None, :]
    )


def shards(
    example_token_inputs,
    example_token_cotangents,
    query_token_inputs,
    query_token_cotangents,
    example_token_lengths,
    query_token_lengths,
    adapter_down_snapshots,
    adapter_up_snapshots,
    down_first_moment,
    down_second_moment,
    up_first_moment,
    up_second_moment,
    snapshot_learning_rates,
):
    demo_x = example_token_inputs[0]
    demo_g = example_token_cotangents[0]
    query_x = query_token_inputs[0]
    query_g = query_token_cotangents[0]
    slots = demo_x.shape[1]
    adapter_down_weight = adapter_down_snapshots[0]
    adapter_up_weight = adapter_up_snapshots[0]
    demo_proj = local_projections(demo_x, demo_g, adapter_down_weight, adapter_up_weight)
    query_proj = local_projections(query_x, query_g, adapter_down_weight, adapter_up_weight)
    demo_proj, query_proj = lax.psum((demo_proj, query_proj), "par")
    demo_weighted = weigh(demo_proj, example_token_lengths, slots)
    query_weighted = weigh(query_proj, query_token_lengths, slots)
    demo_grads = example_gradients(demo_x, demo_g, demo_weighted)
    query_grads = example_gradients(query_x, query_g, query_weighted).astype(jnp.bfloat16)
    first_moment = jnp.concatenate(
        [down_first_moment[0].reshape(-1), up_first_moment[0].reshape(-1)]
    )
    second_moment = jnp.concatenate(
        [down_second_moment[0].reshape(-1), up_second_moment[0].reshape(-1)]
    )
    adjusted = (ADAM_ONE * first_moment[None, :] + (1.0 - ADAM_ONE) * demo_grads) / (
        jnp.sqrt(ADAM_TWO * second_moment[None, :] + (1.0 - ADAM_TWO) * demo_grads * demo_grads)
        + ADAM_EPS
    )
    adjusted = adjusted.astype(jnp.bfloat16)
    piece = lax.all_gather(query_grads, "ex", axis=0, tiled=True)
    block = lax.dot_general(
        adjusted, piece, (((1,), (1,)), ((), ())), preferred_element_type=jnp.float32
    )
    products = block
    piece_norms = jnp.sum(jnp.square(piece.astype(jnp.float32)), axis=1)
    query_norms = piece_norms
    products, query_norms = (products, query_norms)
    demo_norms = jnp.sum(jnp.square(adjusted.astype(jnp.float32)), axis=1)
    learning = snapshot_learning_rates[0]
    demo_norms, query_norms = lax.psum((demo_norms, query_norms), "par")
    return lax.psum(normalized(products, demo_norms, query_norms, learning), ("ckpt", "par"))


def solution(mesh):
    in_specs = (
        P("ckpt", "ex", None, "par"),
        P("ckpt", "ex", None, "par"),
        P("ckpt", "ex", None, "par"),
        P("ckpt", "ex", None, "par"),
        P("ex"),
        P("ex"),
        P("ckpt", "par", None),
        P("ckpt", None, "par"),
        P("ckpt", "par", None),
        P("ckpt", "par", None),
        P("ckpt", None, "par"),
        P("ckpt", None, "par"),
        P("ckpt"),
    )
    out_specs = P("ex", None)
    return jax.shard_map(shards, mesh=mesh, in_specs=in_specs, out_specs=out_specs, check_vma=False)
```

profile of v0, /device:TPU:1, one launch (start us, length us, event | category | flops | bytes accessed | tf_op | source)
XLA Modules:
  0.0 648.0 jit_solution(11157446540569881220)
XLA Ops:
  6.6 2.1 fusion.26
  9.0 0.6 fusion.30
  10.0 1.3 pad_maximum_fusion
  11.3 0.8 pad_maximum_fusion.1
  12.4 219.6 %all-reduce.4.cloned.1.call-done = (f32[3072,128]{0,1:T(8,128)}, f32[1024,128]{0,1:T(8,128)}) async-done(((f32[3072,128]{0,1:T(8,128)}, f32[1024,128]{0,1:T(8,128)}), (f32[3072,128]{0,1:T(8,128)}, f32[1024,128]{0,1:T(8,128)})) %all-reduce.4.cloned.1.call-update) | async-done | bytes 2097168 | tf_op jit(solution)/shard_map/psum | solution.py:78
  232.0 1.1 fusion.21
  233.7 0.5 reshape.120
  234.5 0.9 pad_maximum_fusion.2
  235.8 0.9 copy.38
  236.7 0.9 copy.41
  238.4 0.7 maximum_multiply_fusion
  239.6 0.4 fusion.9
  239.9 2.3 copy.28
  242.2 3.6 reshape.117
  245.8 0.4 fusion.5
  246.2 0.9 copy.40
  247.1 0.5 copy-done.2
  247.8 0.8 copy-done.6
  248.7 1.9 multiply_reduce_fusion.1
  250.6 82.9 %all-gather.2.cloned.1.call-done = bf16[64,32768]{1,0:T(8,128)(2,1)} async-done(((bf16[8,32768]{1,0:T(8,128)(2,1)}), bf16[64,32768]{1,0:T(8,128)(2,1)}) %all-gather.2.cloned.1.call-update) | async-done | bytes 4194320 | tf_op jit(solution)/shard_map/all_gather | solution.py:94
  333.5 3.1 multiply_reduce_fusion
  336.6 47.3 %all-reduce = (f32[64]{0:T(128)S(1)}, f32[24]{0:T(128)S(1)}) all-reduce(f32[64]{0:T(128)S(1)} %multiply_reduce_fusion, f32[24]{0:T(128)S(1)} %get-tuple-element.9), channel_id=1, replica_groups=mesh['ckpt'=2,'ex'=8,'par'=32] {'par'}, use_global_device_ids=true, to_apply=%region_7.8 | all-reduce | flops 88 | bytes 704 | tf_op jit(solution)/shard_map/psum | solution.py:104
  383.9 3.4 fusion.15
  387.3 253.9 %psum.39 = f32[24,64]{1,0:T(8,128)} all-reduce(f32[24,64]{1,0:T(8,128)S(1)} %fusion.15), channel_id=1, replica_groups=mesh['ckpt'=2,'ex'=8,'par'=32] {'ckpt','par'}, use_global_device_ids=true, to_apply=%region_8.9 | all-reduce | flops 1536 | bytes 12288 | tf_op jit(solution)/shard_map/psum | solution.py:105
  (55 shorter events, 3.0 us)
Async XLA Ops:
  6.5 2.5 copy-start
  6.5 2.2 copy-start.8
  6.5 2.2 copy-start.4
  6.5 225.4 %all-reduce.4.cloned.1.call-start = ((), (), s32[]{:S(2)}) async-start(), calls=%async_computation.1 | async-start | bytes 4194304 | tf_op jit(solution)/shard_map/psum | solution.py:78
  6.5 2.5 copy-start.9
  8.7 1.0 copy-start.3
  11.3 0.9 copy-start.12
  12.2 321.3 %all-gather.2.cloned.1.call-start = ((), (), s32[]{:S(2)}) async-start(), calls=%async_computation | async-start | bytes 4718592 | tf_op jit(solution)/shard_map/all_gather | solution.py:94
  234.1 1.3 copy-start.10
  234.1 1.5 copy-start.11
  234.4 3.9 copy-start.13
  234.5 4.6 copy-start.5
  242.2 3.6 copy-start.1
  246.2 1.4 copy-start.2
  247.7 0.9 copy-start.6
  247.7 1.0 copy-start.7
Sparse Core Ops, SparseCore 0:
  12.3 219.5 all-reduce.3
  235.6 97.8 all-gather.1
where the time goes:
time: 652 us; the launch traced here: 648 us
  waiting for transfers between devices  303 us (46%)
  blocking collectives  301 us (46%)
  between operations  14.4 us (2%)
  local copies, waits for them, and re-layouts  11.8 us (2%)
  other arithmetic  10.2 us (2%)
  matrix products  7.83 us (1%)
    psum x1, blocking collectives, shards(): lax.psum(normalized(products, demo_norms, query_norms, learning), ('ckpt'...  254 us
    psum x1, waiting for transfers between devices, shards(): demo_proj, query_proj = lax.psum((demo_proj, query_proj), 'par')  220 us
    all_gather x1, waiting for transfers between devices, shards(): piece = lax.all_gather(query_grads, 'ex', axis=0, tiled=True)  82.9 us
    psum x1, blocking collectives, shards(): demo_norms, query_norms = lax.psum((demo_norms, query_norms), 'par')  47.3 us
  transfers between devices with their start and end apart: 2, of which 2 were waited for; matrix products, arithmetic and copies ran while one was open for 2% of the time, Pallas kernels for 0%

commit v1 on v0

v1 whole, which is shorter than its diff:
```python
import jax
import jax.numpy as jnp
from jax import lax
from jax.experimental import pallas as pl
from jax.experimental.pallas import tpu as pltpu
from jax.sharding import PartitionSpec as P

ADAM_ONE = 0.9
ADAM_TWO = 0.999
ADAM_EPS = 1e-08
NORM_EPS = 1e-06

MESH = pl.DeviceIdType.MESH
F32 = jnp.float32
BF16 = jnp.bfloat16
EXACT = lax.Precision.HIGHEST

RINGS = 16
CORES = 2
ROWS = 4
EX = 8
DEMOS = 24
QUERIES = 8
RANKS = 64
PAIR = 2 * RANKS
TOKENS = 128
FEATURES = 256
LANES = 128
Q_HALF = QUERIES * PAIR // CORES
D_HALF = DEMOS * PAIR // CORES
Q_UNIT = Q_HALF // RINGS
D_UNIT = D_HALF // RINGS
GRAIN = 32


def nt(a, b, precision=None):
    return lax.dot_general(a, b, (((1,), (1,)), ((), ())), precision=precision, preferred_element_type=F32)


def nn(a, b, precision=None):
    return lax.dot_general(a, b, (((1,), (0,)), ((), ())), precision=precision, preferred_element_type=F32)


def iota(shape, axis):
    return lax.broadcasted_iota(jnp.int32, shape, axis)


def kernel(
    xq_h, gq_h, xd_h, gd_h, ad_h, au_h, md_h, vd_h, mu_h, vu_h, qlen, dlen, rate,
    out,
    xq, gq, xd, gd, ad, au, md, vd, mu, vu,
    adt, mom, vel,
    pq, pq_in, pd, pd_in,
    rq, rq_in, rd, rd_in,
    hq, hd,
    qs, us, qall, norms,
    fin_out, fin_in, fin_mine, fin_slots, fin_part, fin_ends,
    load_sem, core_send, core_recv, z_send, z_recv, q_send, q_recv, end_send, end_recv,
):
    me = lax.axis_index("par")
    z, c = lax.div(me, CORES), lax.rem(me, CORES)
    e = lax.axis_index("ex")
    y, x = lax.div(e, 2), lax.rem(e, 2)
    ckpt = lax.axis_index("ckpt")
    other = 1 - c
    core_peer = {"par": 2 * z + other}
    up = {"ex": 2 * lax.rem(y + 1, ROWS) + x}
    down = {"ex": 2 * lax.rem(y + ROWS - 1, ROWS) + x}
    across = {"ex": 2 * y + 1 - x}
    ckpt_peer = {"ckpt": 1 - ckpt}
    far_peer = {"ckpt": 1 - ckpt, "par": 2 * z + other}

    def z_peer(k):
        return lax.rem(z + k, RINGS)

    barrier = pltpu.get_barrier_semaphore()

    def greet(k, carry):
        pl.semaphore_signal(barrier, inc=1, device_id={"par": 2 * z_peer(k) + c}, device_id_type=MESH)
        return carry

    lax.fori_loop(1, RINGS, greet, 0)
    for peer in (core_peer, up, down, across, ckpt_peer, far_peer):
        pl.semaphore_signal(barrier, inc=1, device_id=peer, device_id_type=MESH)

    loads = [
        pltpu.make_async_copy(src, dst, load_sem.at[n])
        for n, (src, dst) in enumerate(
            ((ad_h, ad), (au_h, au), (xq_h, xq), (gq_h, gq), (xd_h, xd), (gd_h, gd), (md_h, md), (vd_h, vd), (mu_h, mu), (vu_h, vu))
        )
    ]
    for load in loads:
        load.start()

    def project(count, xs, gs, to):
        def body(i, carry):
            at = pl.multiple_of(i * 2 * TOKENS, 2 * TOKENS)
            h = nt(adt[...], xs[pl.ds(at, 2 * TOKENS), :])
            k = nt(au[...], gs[pl.ds(at, 2 * TOKENS), :])
            for n in range(2):
                to[pl.ds(at + n * PAIR, RANKS), :] = h[:, n * TOKENS : (n + 1) * TOKENS]
                to[pl.ds(at + n * PAIR + RANKS, RANKS), :] = k[:, n * TOKENS : (n + 1) * TOKENS]
            return carry

        lax.fori_loop(0, count // 2, body, 0)

    loads[0].wait()
    loads[1].wait()
    adt[...] = jnp.transpose(ad[...].astype(F32)).astype(BF16)
    loads[2].wait()
    loads[3].wait()
    project(QUERIES, xq, gq, pq)
    loads[4].wait()
    loads[5].wait()
    project(DEMOS, xd, gd, pd)
    for n in (6, 7, 8, 9):
        loads[n].wait()
    mom[0:RANKS, :] = ADAM_ONE * jnp.transpose(md[...])
    vel[0:RANKS, :] = ADAM_TWO * jnp.transpose(vd[...])
    mom[RANKS:, :] = ADAM_ONE * mu[...]
    vel[RANKS:, :] = ADAM_TWO * vu[...]

    pl.semaphore_wait(barrier, RINGS - 1 + 6)

    def to_core(n, src, dst):
        return pltpu.make_async_remote_copy(src, dst, core_send.at[n], core_recv.at[n], device_id=core_peer, device_id_type=MESH)

    q_cross = to_core(0, pq.at[pl.ds(pl.multiple_of(other * Q_HALF, Q_HALF), Q_HALF)], pq_in)
    d_cross = to_core(1, pd.at[pl.ds(pl.multiple_of(other * D_HALF, D_HALF), D_HALF)], pd_in)
    q_cross.start()
    d_cross.start()

    def fold(half, own, came, send, step):
        def body(i, carry):
            at = pl.multiple_of(i * step, step)
            total = own[pl.ds(pl.multiple_of(c * half + at, step), step), :] + came[pl.ds(at, step), :]
            came[pl.ds(at, step), :] = total
            send[pl.ds(at, step), :] = total.astype(BF16)
            return carry

        lax.fori_loop(0, half // step, body, 0)

    def scatter(n, unit, send, slots):
        def body(k, carry):
            to = z_peer(k)
            pltpu.make_async_remote_copy(
                send.at[pl.ds(pl.multiple_of(to * unit, unit), unit)],
                slots.at[z],
                z_send.at[n],
                z_recv.at[n],
                device_id={"par": 2 * to + c},
                device_id_type=MESH,
            ).start()
            return carry

        lax.fori_loop(1, RINGS, body, 0)

    def spread(n, unit, ref, at):
        def body(k, carry):
            pltpu.make_async_remote_copy(
                ref.at[pl.ds(at, unit)],
                ref.at[pl.ds(at, unit)],
                z_send.at[n],
                z_recv.at[n],
                device_id={"par": 2 * z_peer(k) + c},
                device_id_type=MESH,
            ).start()
            return carry

        lax.fori_loop(1, RINGS, body, 0)

    def await_bytes(ref, sem):
        pltpu.make_async_copy(ref, ref, sem).wait()

    q_cross.wait()
    fold(Q_HALF, pq, pq_in, rq, 128)
    scatter(0, Q_UNIT, rq, rq_in)
    d_cross.wait()
    fold(D_HALF, pd, pd_in, rd, 128)

    def gather_sum(n, unit, own, slots):
        await_bytes(slots.at[pl.ds(0, RINGS - 1)], z_recv.at[n])
        total = own[pl.ds(pl.multiple_of(z * unit, unit), unit), :]

        def body(k, total):
            return total + slots[z_peer(k)].astype(F32)

        return lax.fori_loop(1, RINGS, body, total)

    def weigh(rows, length):
        position = iota((1, TOKENS), 1)
        weight = jnp.where(position < length, 1.0 / jnp.full((1, TOKENS), length, F32), 0.0)
        return (rows * weight).astype(BF16)

    q_total = gather_sum(0, Q_UNIT, pq_in, rq_in)
    q_at = pl.multiple_of(c * Q_HALF + z * Q_UNIT, Q_UNIT)
    hq[pl.ds(q_at, Q_UNIT), :] = weigh(q_total, qlen[lax.div(c * RINGS + z, PAIR // Q_UNIT)])
    spread(1, Q_UNIT, hq, q_at)
    scatter(2, D_UNIT, rd, rd_in)

    await_bytes(hq.at[pl.ds(0, (RINGS - 1) * Q_UNIT)], z_recv.at[1])
    q_half = hq.at[pl.ds(pl.multiple_of(c * Q_HALF, Q_HALF), Q_HALF)]
    q_share = to_core(2, q_half, q_half)
    q_share.start()
    q_share.wait()

    for j in range(QUERIES):
        tokens = pl.ds(j * TOKENS, TOKENS)
        down_grad = nn(hq[pl.ds(j * PAIR + RANKS, RANKS), :], xq[tokens, :])
        up_grad = nn(hq[pl.ds(j * PAIR, RANKS), :], gq[tokens, :])
        for h in range(2):
            lanes = slice(h * LANES, (h + 1) * LANES)
            qs[h, pl.ds(j, RANKS, stride=QUERIES), :] = down_grad[:, lanes]
            qs[h, pl.ds(RANKS * QUERIES + j, RANKS, stride=QUERIES), :] = up_grad[:, lanes]
    piece_rows = RANKS * QUERIES

    def q_copy(block, piece, to):
        return pltpu.make_async_remote_copy(
            qall.at[block, piece], qall.at[block, piece], q_send.at[0], q_recv.at[block, piece], device_id=to, device_id_type=MESH
        )

    for piece in range(4):
        h, part = piece // 2, piece % 2
        qall[e, piece] = qs[h, pl.ds(part * piece_rows, piece_rows), :].astype(BF16)
        for to in (up, down, across):
            q_copy(e, piece, to).start()

    d_total = gather_sum(2, D_UNIT, pd_in, rd_in)
    d_at = pl.multiple_of(c * D_HALF + z * D_UNIT, D_UNIT)
    for k in range(D_UNIT // GRAIN):
        demo = lax.div((c * RINGS + z) * (D_UNIT // GRAIN) + k, PAIR // GRAIN)
        hd[pl.ds(d_at + k * GRAIN, GRAIN), :] = weigh(d_total[k * GRAIN : (k + 1) * GRAIN], dlen[demo])
    spread(3, D_UNIT, hd, d_at)

    above = 2 * lax.rem(y + 1, ROWS) + x
    below = 2 * lax.rem(y + ROWS - 1, ROWS) + x
    beyond = 2 * lax.rem(y + 2, ROWS) + x
    side = 2 * y + 1 - x
    side_above = 2 * lax.rem(y + 1, ROWS) + 1 - x
    side_below = 2 * lax.rem(y + ROWS - 1, ROWS) + 1 - x
    side_beyond = 2 * lax.rem(y + 2, ROWS) + 1 - x

    def arrived(block, piece):
        await_bytes(qall.at[block, piece], q_recv.at[block, piece])

    for piece in range(4):
        for block in (side, above, below):
            arrived(block, piece)
        if piece < 2:
            q_copy(above, piece, down).start()
            q_copy(side, piece, up).start()
            q_copy(side, piece, down).start()
        else:
            q_copy(below, piece, up).start()
            q_copy(above, piece, across).start()
            q_copy(below, piece, across).start()
    arrived(beyond, 0)
    q_copy(beyond, 0, across).start()
    arrived(side_above, 1)
    q_copy(side_above, 1, down).start()
    arrived(side_below, 3)
    q_copy(side_below, 3, up).start()
    arrived(beyond, 2)
    q_copy(beyond, 2, across).start()

    await_bytes(hd.at[pl.ds(0, (RINGS - 1) * D_UNIT)], z_recv.at[3])
    d_half = hd.at[pl.ds(pl.multiple_of(c * D_HALF, D_HALF), D_HALF)]
    d_share = to_core(3, d_half, d_half)
    d_share.start()
    d_share.wait()

    norms[...] = jnp.zeros_like(norms)

    def update(i, carry):
        tokens = pl.ds(pl.multiple_of(i * TOKENS, TOKENS), TOKENS)
        at = pl.multiple_of(i * PAIR, PAIR)
        squares = jnp.zeros((8, LANES), F32)
        for part, first, array in ((0, RANKS, xd), (1, 0, gd)):
            grad = nn(hd[pl.ds(at + first, RANKS), :], array[tokens, :])
            rows = slice(part * RANKS, (part + 1) * RANKS)
            top = mom[rows, :] + (1.0 - ADAM_ONE) * grad
            bottom = jnp.sqrt(vel[rows, :] + (1.0 - ADAM_TWO) * grad * grad) + ADAM_EPS
            adjusted = (top / bottom).astype(BF16).astype(F32)
            for h in range(2):
                piece = adjusted[:, h * LANES : (h + 1) * LANES]
                us[h, pl.ds(part * RANKS * DEMOS + i, RANKS, stride=DEMOS), :] = piece
                squares += jnp.sum((piece * piece).reshape(RANKS // 8, 8, LANES), axis=0)
        norms[pl.ds(EX * QUERIES + i, 1), :] = jnp.sum(squares, axis=0, keepdims=True)
        return carry

    lax.fori_loop(0, DEMOS, update, 0)

    for block, pieces in ((beyond, (1, 3)), (side_above, (0, 2, 3)), (side_below, (0, 1, 2)), (side_beyond, (0, 1, 2, 3))):
        for piece in pieces:
            arrived(block, piece)

    def query_norms(n, carry):
        def body(i, total):
            rows = qall[n, lax.div(i, 8), pl.ds(pl.multiple_of(lax.rem(i, 8) * 64, 64), 64), :].astype(F32)
            return total + jnp.sum((rows * rows).reshape(8, 8, LANES), axis=0)

        total = lax.fori_loop(0, 32, body, jnp.zeros((8, LANES), F32))
        norms[pl.ds(pl.multiple_of(n * QUERIES, QUERIES), QUERIES), :] = total
        return carry

    lax.fori_loop(0, EX, query_norms, 0)

    def products(part):
        def body(r, total):
            u_at = pl.multiple_of(part * RANKS * DEMOS + r * 2 * DEMOS, 2 * DEMOS)
            q_at = pl.multiple_of(r * 2 * QUERIES, 2 * QUERIES)
            left = jnp.concatenate([us[h, pl.ds(u_at, 2 * DEMOS), :] for h in range(2)], axis=1).astype(BF16)
            right = jnp.concatenate(
                [
                    jnp.concatenate([qall[n, 2 * h + part, pl.ds(q_at, 2 * QUERIES), :] for n in range(EX)], axis=0)
                    for h in range(2)
                ],
                axis=1,
            )
            return total + nt(left, right)

        return body

    total = jnp.zeros((2 * DEMOS, 2 * EX * QUERIES), F32)
    for part in range(2):
        total = lax.fori_loop(0, RANKS // 2, products(part), total)

    second = lax.rem(lax.div(iota((DEMOS, LANES), 1), QUERIES), 2) == 1
    folded = jnp.where(second, total[DEMOS:], total[:DEMOS])
    source, target = iota((LANES, LANES), 0), lax.rem(iota((LANES, LANES), 1), EX * QUERIES)
    picks = (lax.div(source, 2 * QUERIES) == lax.div(target, QUERIES)) & (lax.rem(source, QUERIES) == lax.rem(target, QUERIES))
    twice = nn(folded, picks.astype(F32), EXACT)
    sums = nt(jnp.ones((8, LANES), F32), norms[...], EXACT)
    left_lanes = iota((8, LANES), 1) < LANES // 2
    row = iota((8, LANES), 0)

    def packed(core):
        chosen, at = iota((8, DEMOS), 0), iota((8, DEMOS), 1)
        first = ((chosen + 12 * core) == at) & (chosen < 6)
        last = ((chosen + 12 * core + 6) == at) & (chosen < 6)
        body = jnp.where(left_lanes, nn(first.astype(F32), twice, EXACT), nn(last.astype(F32), twice, EXACT))
        return jnp.where(row == 6, sums, body)

    fin_out[...] = packed(other)
    cross = to_core(4, fin_out, fin_in)
    cross.start()
    mine = packed(c)
    cross.wait()
    fin_slots[z] = mine + fin_in[...]
    spread_at = fin_slots.at[z]

    def finish(k, carry):
        pltpu.make_async_remote_copy(
            spread_at, spread_at, z_send.at[4], z_recv.at[4], device_id={"par": 2 * z_peer(k) + c}, device_id_type=MESH
        ).start()
        return carry

    lax.fori_loop(1, RINGS, finish, 0)
    await_bytes(fin_slots.at[pl.ds(0, RINGS - 1)], z_recv.at[4])
    whole = fin_slots[0]
    for n in range(1, RINGS):
        whole = whole + fin_slots[n]

    scale = lax.rsqrt(whole[6:7, :] + NORM_EPS)
    by_query = jnp.where(left_lanes, scale, pltpu.roll(jnp.broadcast_to(scale, (8, LANES)), LANES // 2, 1))
    lane = iota((8, LANES), 1)
    at = EX * QUERIES + 12 * c + row
    by_first = jnp.sum(jnp.where((lane == at) & (row < 6), scale, 0.0), axis=1, keepdims=True)
    by_last = jnp.sum(jnp.where((lane == at + 6) & (row < 6), scale, 0.0), axis=1, keepdims=True)
    scores = rate[0] * whole * jnp.where(left_lanes, by_first, by_last) * by_query
    fin_mine[...] = jnp.where(row < 6, scores, 0.0)

    ends = [
        pltpu.make_async_remote_copy(fin_mine, fin_ends.at[n], end_send.at[n], end_recv.at[n], device_id=to, device_id_type=MESH)
        for n, to in enumerate((ckpt_peer, core_peer, far_peer))
    ]
    for copy in ends:
        copy.start()
    for copy in ends:
        copy.wait()
    fin_part[c] = fin_mine[...] + fin_ends[0]
    fin_part[other] = fin_ends[1] + fin_ends[2]
    both = jnp.concatenate([fin_part[0], fin_part[1]], axis=0)
    demo, at = iota((DEMOS, 16), 0), iota((DEMOS, 16), 1)
    rows = nn((at == 8 * lax.div(demo, 12) + lax.rem(demo, 6)).astype(F32), both, EXACT)
    late = lax.rem(lax.div(iota((DEMOS, LANES // 2), 0), 6), 2) == 1
    out[...] = jnp.where(late, rows[:, LANES // 2 :], rows[:, : LANES // 2])

    await_bytes(rq.at[pl.ds(0, (RINGS - 1) * Q_UNIT)], z_send.at[0])
    await_bytes(hq.at[pl.ds(0, (RINGS - 1) * Q_UNIT)], z_send.at[1])
    await_bytes(rd.at[pl.ds(0, (RINGS - 1) * D_UNIT)], z_send.at[2])
    await_bytes(hd.at[pl.ds(0, (RINGS - 1) * D_UNIT)], z_send.at[3])
    await_bytes(fin_slots.at[pl.ds(0, RINGS - 1)], z_send.at[4])
    await_bytes(qall.at[pl.ds(0, EX - 1)], q_send.at[0])


def shards(
    example_token_inputs,
    example_token_cotangents,
    query_token_inputs,
    query_token_cotangents,
    example_token_lengths,
    query_token_lengths,
    adapter_down_snapshots,
    adapter_up_snapshots,
    down_first_moment,
    down_second_moment,
    up_first_moment,
    up_second_moment,
    snapshot_learning_rates,
):
    anywhere, scalars = pl.BlockSpec(memory_space=pl.ANY), pl.BlockSpec(memory_space=pltpu.SMEM)
    vmem = pltpu.VMEM
    dma = pltpu.SemaphoreType.DMA
    return pl.pallas_call(
        kernel,
        out_shape=jax.ShapeDtypeStruct((DEMOS, EX * QUERIES), F32),
        in_specs=[anywhere] * 10 + [scalars] * 3,
        out_specs=pl.BlockSpec(memory_space=vmem),
        scratch_shapes=[
            vmem((QUERIES * TOKENS, FEATURES), BF16),
            vmem((QUERIES * TOKENS, FEATURES), BF16),
            vmem((DEMOS * TOKENS, FEATURES), BF16),
            vmem((DEMOS * TOKENS, FEATURES), BF16),
            vmem((FEATURES, RANKS), BF16),
            vmem((RANKS, FEATURES), BF16),
            vmem((FEATURES, RANKS), F32),
            vmem((FEATURES, RANKS), F32),
            vmem((RANKS, FEATURES), F32),
            vmem((RANKS, FEATURES), F32),
            vmem((RANKS, FEATURES), BF16),
            vmem((PAIR, FEATURES), F32),
            vmem((PAIR, FEATURES), F32),
            vmem((QUERIES * PAIR, TOKENS), F32),
            vmem((Q_HALF, TOKENS), F32),
            vmem((DEMOS * PAIR, TOKENS), F32),
            vmem((D_HALF, TOKENS), F32),
            vmem((Q_HALF, TOKENS), BF16),
            vmem((RINGS, Q_UNIT, TOKENS), BF16),
            vmem((D_HALF, TOKENS), BF16),
            vmem((RINGS, D_UNIT, TOKENS), BF16),
            vmem((QUERIES * PAIR, TOKENS), BF16),
            vmem((DEMOS * PAIR, TOKENS), BF16),
            vmem((2, PAIR * QUERIES, LANES), F32),
            vmem((2, PAIR * DEMOS, LANES), F32),
            vmem((EX, 4, RANKS * QUERIES, LANES), BF16),
            vmem((LANES, LANES), F32),
            vmem((8, LANES), F32),
            vmem((8, LANES), F32),
            vmem((8, LANES), F32),
            vmem((RINGS, 8, LANES), F32),
            vmem((2, 8, LANES), F32),
            vmem((3, 8, LANES), F32),
            dma((10,)),
            dma((5,)),
            dma((5,)),
            dma((5,)),
            dma((5,)),
            dma((1,)),
            dma((EX, 4)),
            dma((3,)),
            dma((3,)),
        ],
        compiler_params=pltpu.CompilerParams(collective_id=0, has_side_effects=True, vmem_limit_bytes=40 * 2**20),
    )(
        query_token_inputs.reshape(QUERIES * TOKENS, FEATURES),
        query_token_cotangents.reshape(QUERIES * TOKENS, FEATURES),
        example_token_inputs.reshape(DEMOS * TOKENS, FEATURES),
        example_token_cotangents.reshape(DEMOS * TOKENS, FEATURES),
        adapter_down_snapshots[0],
        adapter_up_snapshots[0],
        down_first_moment[0],
        down_second_moment[0],
        up_first_moment[0],
        up_second_moment[0],
        query_token_lengths,
        example_token_lengths,
        snapshot_learning_rates,
    )


def solution(mesh):
    in_specs = (
        P("ckpt", "ex", None, "par"),
        P("ckpt", "ex", None, "par"),
        P("ckpt", "ex", None, "par"),
        P("ckpt", "ex", None, "par"),
        P("ex"),
        P("ex"),
        P("ckpt", "par", None),
        P("ckpt", None, "par"),
        P("ckpt", "par", None),
        P("ckpt", "par", None),
        P("ckpt", None, "par"),
        P("ckpt", None, "par"),
        P("ckpt"),
    )
    out_specs = P("ex", None)
    return jax.shard_map(shards, mesh=mesh, in_specs=in_specs, out_specs=out_specs, check_vma=False)
```

time: 652 us -> 124 us (0.19)
  waiting for transfers between devices: 303 us -> 0 us
  blocking collectives: 301 us -> 0 us
  Pallas kernels: 0 us -> 110 us
  between operations: 14.4 us -> 0.69 us
  other arithmetic: 10.2 us -> 0 us
  matrix products: 7.83 us -> 0 us
    psum x2 -> x0, blocking collectives: 301 us -> none  [the longest x1 254 us: shards(): lax.psum(normalized(products, demo_norms, query_norms, learning), ('ckpt'...]
    psum x1 -> x0, waiting for transfers between devices: 220 us -> none  [shards(): demo_proj, query_proj = lax.psum((demo_proj, query_proj), 'par')]
    pallas_call x0 -> x1, Pallas kernels: none -> 110 us  [shards(): pl.pallas_call(kernel, out_shape=jax.ShapeDtypeStruct((DEMOS, EX * QUERIE...]
    all_gather x1 -> x0, waiting for transfers between devices: 82.9 us -> none  [shards(): piece = lax.all_gather(query_grads, 'ex', axis=0, tiled=True)]
    dot_general x9 -> x0, matrix products: 7.83 us -> none  [the longest x1 3.39 us: shards(): lax.dot_general(adjusted, piece, (((1,), (1,)), ((), ())), preferred_elem...]
    unnamed x37 -> x22, local copies, waits for them, and re-layouts: 4.83 us -> 12 us
  transfers between devices with their start and end apart: 2 -> 0, of which waited for: 2 -> 0; matrix products, arithmetic and copies ran while one was open for 2% -> 0% of each run, Pallas kernels for 0% -> 0%
where the time goes in v1:
time: 124 us; the launch traced here: 123 us
  Pallas kernels  110 us (89%)
  local copies, waits for them, and re-layouts  12 us (10%)
    pallas_call x1, Pallas kernels, shards(): pl.pallas_call(kernel, out_shape=jax.ShapeDtypeStruct((DEMOS, EX * QUERIE...  110 us
    unnamed x22, local copies, waits for them, and re-layouts  12 us

profile of v1, /device:TPU:1, one launch (start us, length us, event | category | flops | bytes accessed | tf_op | source)
XLA Modules:
  0.0 123.0 jit_solution(11755297211369644275)
XLA Ops:
  0.7 0.9 copy.14
  1.5 0.9 copy.15
  2.5 0.9 copy.16
  3.4 0.0 copy-start
  3.4 1.4 %copy-done = bf16[1,24,128,256]{3,2,1,0:T(8,128)(2,1)S(1)} copy-done((bf16[1,24,128,256]{3,2,1,0:T(8,128)(2,1)S(1)}, bf16[1,24,128,256]{3,2,1,0:T(8,128)(2,1)}, u32[]{:S(2)}) %copy-start) | copy-done | bytes 1572888
  4.8 0.0 copy-start.1
  4.8 1.4 %copy-done.1 = bf16[1,24,128,256]{3,2,1,0:T(8,128)(2,1)S(1)} copy-done((bf16[1,24,128,256]{3,2,1,0:T(8,128)(2,1)S(1)}, bf16[1,24,128,256]{3,2,1,0:T(8,128)(2,1)}, u32[]{:S(2)}) %copy-start.1) | copy-done | bytes 1572888
  6.2 0.0 copy-start.2
  6.2 1.0 copy-done.2
  7.3 0.0 copy-start.3
  7.3 1.0 copy-done.3
  8.3 0.0 copy-start.4
  8.3 0.8 copy-done.4
  9.2 0.0 copy-start.5
  9.2 0.8 copy-done.5
  10.0 0.0 copy-start.6
  10.0 0.8 copy-done.6
  10.8 0.0 copy-start.7
  10.8 0.7 copy-done.7
  11.4 0.0 copy-start.8
  11.4 0.7 copy-done.8
  12.1 110.3 %shard_map.127 = f32[24,64]{1,0:T(8,128)S(1)} custom-call(bf16[1024,256]{1,0:T(8,128)(2,1)S(1)} %bitcast.12, bf16[1024,256]{1,0:T(8,128)(2,1)S(1)} %bitcast.13, bf16[3072,256]{1,0:T(8,128)(2,1)S(1)} %bitcast.10, bf16[3072,256]{1,0:T(8,128)(2,1)S(1)} %bitcast.11, bf16[256,64]{1,0:T(8,128)(2,1)S(1)} %bitcast.16, bf16[64,256]{1,0:T(8,128)(2,1)S(1)} %bitcast.19, ...), custom_call_target="tpu_custom_call" | custom-call | tf_op jit(solution)/shard_map/pallas_call | solution.py:415
  122.4 0.6 copy.19
Async XLA Ops:
  3.4 1.4 %copy-start = (bf16[1,24,128,256]{3,2,1,0:T(8,128)(2,1)S(1)}, bf16[1,24,128,256]{3,2,1,0:T(8,128)(2,1)}, u32[]{:S(2)}) copy-start(bf16[1,24,128,256]{3,2,1,0:T(8,128)(2,1)} %param.13) | copy-start | bytes 4718596
  4.8 1.4 %copy-start.1 = (bf16[1,24,128,256]{3,2,1,0:T(8,128)(2,1)S(1)}, bf16[1,24,128,256]{3,2,1,0:T(8,128)(2,1)}, u32[]{:S(2)}) copy-start(bf16[1,24,128,256]{3,2,1,0:T(8,128)(2,1)} %param.14) | copy-start | bytes 4718596
  6.2 1.0 copy-start.2
  7.3 1.0 copy-start.3
  8.3 0.8 copy-start.4
  9.2 0.8 copy-start.5
  10.0 0.8 copy-start.6
  10.8 0.7 copy-start.7
  11.4 0.7 copy-start.8

commit v2 on v1

--- a/solution.py
+++ b/solution.py
@@ -30,7 +30,10 @@
 D_HALF = DEMOS * PAIR // CORES
 Q_UNIT = Q_HALF // RINGS
 D_UNIT = D_HALF // RINGS
-GRAIN = 32
+D_SIDE = D_UNIT // 2
+D_CLASS = D_HALF // 2
+CLASS = RINGS // 2
+GRAIN = 16
 
 
 def nt(a, b, precision=None):
@@ -49,9 +52,9 @@
     xq_h, gq_h, xd_h, gd_h, ad_h, au_h, md_h, vd_h, mu_h, vu_h, qlen, dlen, rate,
     out,
     xq, gq, xd, gd, ad, au, md, vd, mu, vu,
-    adt, mom, vel,
+    mom, vel,
     pq, pq_in, pd, pd_in,
-    rq, rq_in, rd, rd_in,
+    rq, rq_in, rd, rd_in, re, re_in,
     hq, hd,
     qs, us, qall, norms,
     fin_out, fin_in, fin_mine, fin_slots, fin_part, fin_ends,
@@ -73,6 +76,9 @@
     def z_peer(k):
         return lax.rem(z + k, RINGS)
 
+    def far_first(i, count):
+        return count // 2 + (2 * lax.rem(i, 2) - 1) * lax.div(i + 1, 2)
+
     barrier = pltpu.get_barrier_semaphore()
 
     def greet(k, carry):
@@ -95,7 +101,7 @@
     def project(count, xs, gs, to):
         def body(i, carry):
             at = pl.multiple_of(i * 2 * TOKENS, 2 * TOKENS)
-            h = nt(adt[...], xs[pl.ds(at, 2 * TOKENS), :])
+            h = nt(ad[...], xs[pl.ds(at, 2 * TOKENS), :])
             k = nt(au[...], gs[pl.ds(at, 2 * TOKENS), :])
             for n in range(2):
                 to[pl.ds(at + n * PAIR, RANKS), :] = h[:, n * TOKENS : (n + 1) * TOKENS]
@@ -106,29 +112,16 @@
 
     loads[0].wait()
     loads[1].wait()
-    adt[...] = jnp.transpose(ad[...].astype(F32)).astype(BF16)
     loads[2].wait()
     loads[3].wait()
     project(QUERIES, xq, gq, pq)
-    loads[4].wait()
-    loads[5].wait()
-    project(DEMOS, xd, gd, pd)
-    for n in (6, 7, 8, 9):
-        loads[n].wait()
-    mom[0:RANKS, :] = ADAM_ONE * jnp.transpose(md[...])
-    vel[0:RANKS, :] = ADAM_TWO * jnp.transpose(vd[...])
-    mom[RANKS:, :] = ADAM_ONE * mu[...]
-    vel[RANKS:, :] = ADAM_TWO * vu[...]
-
     pl.semaphore_wait(barrier, RINGS - 1 + 6)
 
     def to_core(n, src, dst):
         return pltpu.make_async_remote_copy(src, dst, core_send.at[n], core_recv.at[n], device_id=core_peer, device_id_type=MESH)
 
     q_cross = to_core(0, pq.at[pl.ds(pl.multiple_of(other * Q_HALF, Q_HALF), Q_HALF)], pq_in)
-    d_cross = to_core(1, pd.at[pl.ds(pl.multiple_of(other * D_HALF, D_HALF), D_HALF)], pd_in)
     q_cross.start()
-    d_cross.start()
 
     def fold(half, own, came, send, step):
         def body(i, carry):
@@ -141,8 +134,8 @@
         lax.fori_loop(0, half // step, body, 0)
 
     def scatter(n, unit, send, slots):
-        def body(k, carry):
-            to = z_peer(k)
+        def body(i, carry):
+            to = z_peer(far_first(i, RINGS))
             pltpu.make_async_remote_copy(
                 send.at[pl.ds(pl.multiple_of(to * unit, unit), unit)],
                 slots.at[z],
@@ -153,21 +146,21 @@
             ).start()
             return carry
 
-        lax.fori_loop(1, RINGS, body, 0)
+        lax.fori_loop(0, RINGS - 1, body, 0)
 
     def spread(n, unit, ref, at):
-        def body(k, carry):
+        def body(i, carry):
             pltpu.make_async_remote_copy(
                 ref.at[pl.ds(at, unit)],
                 ref.at[pl.ds(at, unit)],
                 z_send.at[n],
                 z_recv.at[n],
-                device_id={"par": 2 * z_peer(k) + c},
+                device_id={"par": 2 * z_peer(far_first(i, RINGS)) + c},
                 device_id_type=MESH,
             ).start()
             return carry
 
-        lax.fori_loop(1, RINGS, body, 0)
+        lax.fori_loop(0, RINGS - 1, body, 0)
 
     def await_bytes(ref, sem):
         pltpu.make_async_copy(ref, ref, sem).wait()
@@ -175,8 +168,40 @@
     q_cross.wait()
     fold(Q_HALF, pq, pq_in, rq, 128)
     scatter(0, Q_UNIT, rq, rq_in)
+    loads[4].wait()
+    loads[5].wait()
+    project(DEMOS, xd, gd, pd)
+    d_cross = to_core(1, pd.at[pl.ds(pl.multiple_of(other * D_HALF, D_HALF), D_HALF)], pd_in)
+    d_cross.start()
+    for n in (6, 7, 8, 9):
+        loads[n].wait()
+    mom[0:RANKS, :] = ADAM_ONE * md[...]
+    vel[0:RANKS, :] = ADAM_TWO * vd[...]
+    mom[RANKS:, :] = ADAM_ONE * mu[...]
+    vel[RANKS:, :] = ADAM_TWO * vu[...]
+
     d_cross.wait()
     fold(D_HALF, pd, pd_in, rd, 128)
+    parity, place = lax.rem(z, 2), lax.div(z, 2)
+    sides = (lax.rem(z + 1 - 2 * parity, RINGS), lax.rem(z + RINGS - 1 + 2 * parity, RINGS))
+
+    def to_sides(n, src, src_at, dst, dst_at):
+        def body(m, carry):
+            for side, to in enumerate(sides):
+                at = pl.multiple_of(m * D_UNIT + side * D_SIDE, D_SIDE)
+                pltpu.make_async_remote_copy(
+                    src.at[pl.ds(src_at + at, D_SIDE)],
+                    dst.at[pl.ds(dst_at + at, D_SIDE)],
+                    z_send.at[n],
+                    z_recv.at[n],
+                    device_id={"par": 2 * to + c},
+                    device_id_type=MESH,
+                ).start()
+            return carry
+
+        lax.fori_loop(0, CLASS, body, 0)
+
+    to_sides(2, rd, pl.multiple_of((1 - parity) * D_CLASS, D_CLASS), rd_in, 0)
 
     def gather_sum(n, unit, own, slots):
         await_bytes(slots.at[pl.ds(0, RINGS - 1)], z_recv.at[n])
@@ -196,7 +221,34 @@
     q_at = pl.multiple_of(c * Q_HALF + z * Q_UNIT, Q_UNIT)
     hq[pl.ds(q_at, Q_UNIT), :] = weigh(q_total, qlen[lax.div(c * RINGS + z, PAIR // Q_UNIT)])
     spread(1, Q_UNIT, hq, q_at)
-    scatter(2, D_UNIT, rd, rd_in)
+    await_bytes(rd_in, z_recv.at[2])
+
+    def fold_class(i, carry):
+        at = pl.multiple_of(i * D_UNIT, D_UNIT)
+        own = pl.ds(pl.multiple_of(parity * D_CLASS + at, D_UNIT), D_UNIT)
+        total = pd_in[own, :] + rd_in[pl.ds(at, D_UNIT), :].astype(F32)
+        pd_in[own, :] = total
+        re[pl.ds(at, D_UNIT), :] = total.astype(BF16)
+        return carry
+
+    lax.fori_loop(0, CLASS, fold_class, 0)
+
+    def class_peer(i):
+        return lax.rem(place + far_first(i, CLASS), CLASS)
+
+    def to_class(i, carry):
+        m = class_peer(i)
+        pltpu.make_async_remote_copy(
+            re.at[pl.ds(pl.multiple_of(m * D_UNIT, D_UNIT), D_UNIT)],
+            re_in.at[place],
+            z_send.at[3],
+            z_recv.at[3],
+            device_id={"par": 2 * (2 * m + parity) + c},
+            device_id_type=MESH,
+        ).start()
+        return carry
+
+    lax.fori_loop(0, CLASS - 1, to_class, 0)
 
     await_bytes(hq.at[pl.ds(0, (RINGS - 1) * Q_UNIT)], z_recv.at[1])
     q_half = hq.at[pl.ds(pl.multiple_of(c * Q_HALF, Q_HALF), Q_HALF)]
@@ -225,12 +277,23 @@
         for to in (up, down, across):
             q_copy(e, piece, to).start()
 
-    d_total = gather_sum(2, D_UNIT, pd_in, rd_in)
-    d_at = pl.multiple_of(c * D_HALF + z * D_UNIT, D_UNIT)
+    await_bytes(re_in.at[pl.ds(0, CLASS - 1)], z_recv.at[3])
+    d_place = pl.multiple_of(parity * D_CLASS + place * D_UNIT, D_UNIT)
+    d_total = lax.fori_loop(
+        1, CLASS, lambda k, total: total + re_in[lax.rem(place + k, CLASS)].astype(F32), pd_in[pl.ds(d_place, D_UNIT), :]
+    )
+    d_at = pl.multiple_of(c * D_HALF + d_place, D_UNIT)
     for k in range(D_UNIT // GRAIN):
-        demo = lax.div((c * RINGS + z) * (D_UNIT // GRAIN) + k, PAIR // GRAIN)
+        demo = lax.div(lax.div(d_at, GRAIN) + k, PAIR // GRAIN)
         hd[pl.ds(d_at + k * GRAIN, GRAIN), :] = weigh(d_total[k * GRAIN : (k + 1) * GRAIN], dlen[demo])
-    spread(3, D_UNIT, hd, d_at)
+
+    def spread_class(i, carry):
+        ref = hd.at[pl.ds(d_at, D_UNIT)]
+        to = {"par": 2 * (2 * class_peer(i) + parity) + c}
+        pltpu.make_async_remote_copy(ref, ref, z_send.at[5], z_recv.at[5], device_id=to, device_id_type=MESH).start()
+        return carry
+
+    lax.fori_loop(0, CLASS - 1, spread_class, 0)
 
     above = 2 * lax.rem(y + 1, ROWS) + x
     below = 2 * lax.rem(y + ROWS - 1, ROWS) + x
@@ -254,6 +317,9 @@
             q_copy(below, piece, up).start()
             q_copy(above, piece, across).start()
             q_copy(below, piece, across).start()
+    await_bytes(hd.at[pl.ds(0, (CLASS - 1) * D_UNIT)], z_recv.at[5])
+    d_class = pl.multiple_of(c * D_HALF + parity * D_CLASS, D_CLASS)
+    to_sides(6, hd, d_class, hd, d_class)
     arrived(beyond, 0)
     q_copy(beyond, 0, across).start()
     arrived(side_above, 1)
@@ -263,13 +329,23 @@
     arrived(beyond, 2)
     q_copy(beyond, 2, across).start()
 
-    await_bytes(hd.at[pl.ds(0, (RINGS - 1) * D_UNIT)], z_recv.at[3])
+    norms[...] = jnp.zeros_like(norms)
+
+    def query_norms(n, carry):
+        total = jnp.zeros((8, LANES), F32)
+        for piece in range(4):
+            rows = qall[n, piece].astype(F32)
+            total += jnp.sum((rows * rows).reshape(RANKS, QUERIES, LANES), axis=0)
+        norms[pl.ds(pl.multiple_of(n * QUERIES, QUERIES), QUERIES), :] = total
+        return carry
+
+    for block in (e, side, above, below):
+        query_norms(block, 0)
+    await_bytes(hd.at[pl.ds(0, D_CLASS)], z_recv.at[6])
     d_half = hd.at[pl.ds(pl.multiple_of(c * D_HALF, D_HALF), D_HALF)]
     d_share = to_core(3, d_half, d_half)
     d_share.start()
-    d_share.wait()
-
-    norms[...] = jnp.zeros_like(norms)
+
 
     def update(i, carry):
         tokens = pl.ds(pl.multiple_of(i * TOKENS, TOKENS), TOKENS)
@@ -288,42 +364,39 @@
         norms[pl.ds(EX * QUERIES + i, 1), :] = jnp.sum(squares, axis=0, keepdims=True)
         return carry
 
-    lax.fori_loop(0, DEMOS, update, 0)
+    first = c * (DEMOS // CORES)
+    lax.fori_loop(first, first + DEMOS // CORES, update, 0)
+    d_share.wait()
+    first = other * (DEMOS // CORES)
+    lax.fori_loop(first, first + DEMOS // CORES, update, 0)
 
     for block, pieces in ((beyond, (1, 3)), (side_above, (0, 2, 3)), (side_below, (0, 1, 2)), (side_beyond, (0, 1, 2, 3))):
         for piece in pieces:
             arrived(block, piece)
-
-    def query_norms(n, carry):
+        query_norms(block, 0)
+
+    def products(part):
         def body(i, total):
-            rows = qall[n, lax.div(i, 8), pl.ds(pl.multiple_of(lax.rem(i, 8) * 64, 64), 64), :].astype(F32)
-            return total + jnp.sum((rows * rows).reshape(8, 8, LANES), axis=0)
-
-        total = lax.fori_loop(0, 32, body, jnp.zeros((8, LANES), F32))
-        norms[pl.ds(pl.multiple_of(n * QUERIES, QUERIES), QUERIES), :] = total
-        return carry
-
-    lax.fori_loop(0, EX, query_norms, 0)
-
-    def products(part):
-        def body(r, total):
-            u_at = pl.multiple_of(part * RANKS * DEMOS + r * 2 * DEMOS, 2 * DEMOS)
-            q_at = pl.multiple_of(r * 2 * QUERIES, 2 * QUERIES)
-            left = jnp.concatenate([us[h, pl.ds(u_at, 2 * DEMOS), :] for h in range(2)], axis=1).astype(BF16)
-            right = jnp.concatenate(
-                [
-                    jnp.concatenate([qall[n, 2 * h + part, pl.ds(q_at, 2 * QUERIES), :] for n in range(EX)], axis=0)
-                    for h in range(2)
-                ],
-                axis=1,
-            )
-            return total + nt(left, right)
+            for n in range(8):
+                r = i * 8 + n
+                u_at = pl.multiple_of(part * RANKS * DEMOS + r * 2 * DEMOS, 2 * DEMOS)
+                q_at = pl.multiple_of(r * 2 * QUERIES, 2 * QUERIES)
+                left = jnp.concatenate([us[h, pl.ds(u_at, 2 * DEMOS), :] for h in range(2)], axis=1).astype(BF16)
+                right = jnp.concatenate(
+                    [
+                        jnp.concatenate([qall[n, 2 * h + part, pl.ds(q_at, 2 * QUERIES), :] for n in range(EX)], axis=0)
+                        for h in range(2)
+                    ],
+                    axis=1,
+                )
+                total = total + nt(left, right)
+            return total
 
         return body
 
     total = jnp.zeros((2 * DEMOS, 2 * EX * QUERIES), F32)
     for part in range(2):
-        total = lax.fori_loop(0, RANKS // 2, products(part), total)
+        total = lax.fori_loop(0, RANKS // 16, products(part), total)
 
     second = lax.rem(lax.div(iota((DEMOS, LANES), 1), QUERIES), 2) == 1
     folded = jnp.where(second, total[DEMOS:], total[:DEMOS])
@@ -349,13 +422,12 @@
     fin_slots[z] = mine + fin_in[...]
     spread_at = fin_slots.at[z]
 
-    def finish(k, carry):
-        pltpu.make_async_remote_copy(
-            spread_at, spread_at, z_send.at[4], z_recv.at[4], device_id={"par": 2 * z_peer(k) + c}, device_id_type=MESH
-        ).start()
-        return carry
-
-    lax.fori_loop(1, RINGS, finish, 0)
+    def finish(i, carry):
+        to = {"par": 2 * z_peer(far_first(i, RINGS)) + c}
+        pltpu.make_async_remote_copy(spread_at, spread_at, z_send.at[4], z_recv.at[4], device_id=to, device_id_type=MESH).start()
+        return carry
+
+    lax.fori_loop(0, RINGS - 1, finish, 0)
     await_bytes(fin_slots.at[pl.ds(0, RINGS - 1)], z_recv.at[4])
     whole = fin_slots[0]
     for n in range(1, RINGS):
@@ -388,8 +460,10 @@
 
     await_bytes(rq.at[pl.ds(0, (RINGS - 1) * Q_UNIT)], z_send.at[0])
     await_bytes(hq.at[pl.ds(0, (RINGS - 1) * Q_UNIT)], z_send.at[1])
-    await_bytes(rd.at[pl.ds(0, (RINGS - 1) * D_UNIT)], z_send.at[2])
-    await_bytes(hd.at[pl.ds(0, (RINGS - 1) * D_UNIT)], z_send.at[3])
+    await_bytes(rd.at[pl.ds(0, D_CLASS)], z_send.at[2])
+    await_bytes(re_in.at[pl.ds(0, CLASS - 1)], z_send.at[3])
+    await_bytes(hd.at[pl.ds(0, (CLASS - 1) * D_UNIT)], z_send.at[5])
+    await_bytes(hd.at[pl.ds(0, D_CLASS)], z_send.at[6])
     await_bytes(fin_slots.at[pl.ds(0, RINGS - 1)], z_send.at[4])
     await_bytes(qall.at[pl.ds(0, EX - 1)], q_send.at[0])
 
@@ -422,13 +496,12 @@
             vmem((QUERIES * TOKENS, FEATURES), BF16),
             vmem((DEMOS * TOKENS, FEATURES), BF16),
             vmem((DEMOS * TOKENS, FEATURES), BF16),
-            vmem((FEATURES, RANKS), BF16),
             vmem((RANKS, FEATURES), BF16),
-            vmem((FEATURES, RANKS), F32),
-            vmem((FEATURES, RANKS), F32),
+            vmem((RANKS, FEATURES), BF16),
             vmem((RANKS, FEATURES), F32),
             vmem((RANKS, FEATURES), F32),
-            vmem((RANKS, FEATURES), BF16),
+            vmem((RANKS, FEATURES), F32),
+            vmem((RANKS, FEATURES), F32),
             vmem((PAIR, FEATURES), F32),
             vmem((PAIR, FEATURES), F32),
             vmem((QUERIES * PAIR, TOKENS), F32),
@@ -438,7 +511,9 @@
             vmem((Q_HALF, TOKENS), BF16),
             vmem((RINGS, Q_UNIT, TOKENS), BF16),
             vmem((D_HALF, TOKENS), BF16),
-            vmem((RINGS, D_UNIT, TOKENS), BF16),
+            vmem((D_CLASS, TOKENS), BF16),
+            vmem((D_CLASS, TOKENS), BF16),
+            vmem((CLASS, D_UNIT, TOKENS), BF16),
             vmem((QUERIES * PAIR, TOKENS), BF16),
             vmem((DEMOS * PAIR, TOKENS), BF16),
             vmem((2, PAIR * QUERIES, LANES), F32),
@@ -454,23 +529,23 @@
             dma((10,)),
             dma((5,)),
             dma((5,)),
-            dma((5,)),
-            dma((5,)),
+            dma((7,)),
+            dma((7,)),
             dma((1,)),
             dma((EX, 4)),
             dma((3,)),
             dma((3,)),
         ],
-        compiler_params=pltpu.CompilerParams(collective_id=0, has_side_effects=True, vmem_limit_bytes=40 * 2**20),
+        compiler_params=pltpu.CompilerParams(collective_id=0, has_side_effects=True, vmem_limit_bytes=60 * 2**20),
     )(
         query_token_inputs.reshape(QUERIES * TOKENS, FEATURES),
         query_token_cotangents.reshape(QUERIES * TOKENS, FEATURES),
         example_token_inputs.reshape(DEMOS * TOKENS, FEATURES),
         example_token_cotangents.reshape(DEMOS * TOKENS, FEATURES),
-        adapter_down_snapshots[0],
+        adapter_down_snapshots[0].T,
         adapter_up_snapshots[0],
-        down_first_moment[0],
-        down_second_moment[0],
+        down_first_moment[0].T,
+        down_second_moment[0].T,
         up_first_moment[0],
         up_second_moment[0],
         query_token_lengths,

time: 124 us -> 91.9 us (0.74)
  Pallas kernels: 110 us -> 89.8 us
  local copies, waits for them, and re-layouts: 12 us -> 1.31 us
    pallas_call x1, Pallas kernels: 110 us -> 89.8 us  [shards(): pl.pallas_call(kernel, out_shape=jax.ShapeDtypeStruct((DEMOS, EX * QUERIE...]
    unnamed x22 -> x1, local copies, waits for them, and re-layouts: 12 us -> 1.31 us
where the time goes in v2:
time: 91.9 us; the launch traced here: 91.7 us
  Pallas kernels  89.8 us (98%)
  local copies, waits for them, and re-layouts  1.31 us (1%)
    pallas_call x1, Pallas kernels, shards(): pl.pallas_call(kernel, out_shape=jax.ShapeDtypeStruct((DEMOS, EX * QUERIE...  89.8 us

profile of v2, /device:TPU:1, one launch (start us, length us, event | category | flops | bytes accessed | tf_op | source)
XLA Modules:
  0.0 91.7 jit_solution(6323863627524587654)
XLA Ops:
  0.7 89.8 %shard_map.127 = f32[24,64]{1,0:T(8,128)} custom-call(bf16[1024,256]{1,0:T(8,128)(2,1)} %bitcast.18, bf16[1024,256]{1,0:T(8,128)(2,1)} %bitcast.19, bf16[3072,256]{1,0:T(8,128)(2,1)} %bitcast.16, bf16[3072,256]{1,0:T(8,128)(2,1)} %bitcast.17, bf16[64,256]{1,0:T(8,128)(2,1)} %bitcast.24, bf16[64,256]{1,0:T(8,128)(2,1)} %bitcast.25, f32[64,256]{1,0:T(8,128)} %bitcast.20, ...), custom_call_target="tpu_custom_call" | custom-call | tf_op jit(solution)/shard_map/pallas_call | solution.py:489
  90.4 1.3 %copy.16 = f32[24,64]{1,0:T(8,128)} copy(f32[24,64]{1,0:T(8,128)} %shard_map.127) | data formatting | bytes 12288

commit v3 on v2

--- a/solution.py
+++ b/solution.py
@@ -28,7 +28,8 @@
 LANES = 128
 Q_HALF = QUERIES * PAIR // CORES
 D_HALF = DEMOS * PAIR // CORES
-Q_UNIT = Q_HALF // RINGS
+Q_PART = Q_HALF // 2
+Q_UNIT = Q_PART // RINGS
 D_UNIT = D_HALF // RINGS
 D_SIDE = D_UNIT // 2
 D_CLASS = D_HALF // 2
@@ -98,14 +99,14 @@
     for load in loads:
         load.start()
 
-    def project(count, xs, gs, to):
+    def project(count, xs, gs, to, k_row, h_row):
         def body(i, carry):
             at = pl.multiple_of(i * 2 * TOKENS, 2 * TOKENS)
             h = nt(ad[...], xs[pl.ds(at, 2 * TOKENS), :])
             k = nt(au[...], gs[pl.ds(at, 2 * TOKENS), :])
             for n in range(2):
-                to[pl.ds(at + n * PAIR, RANKS), :] = h[:, n * TOKENS : (n + 1) * TOKENS]
-                to[pl.ds(at + n * PAIR + RANKS, RANKS), :] = k[:, n * TOKENS : (n + 1) * TOKENS]
+                to[pl.ds(pl.multiple_of(h_row(2 * i + n), RANKS), RANKS), :] = h[:, n * TOKENS : (n + 1) * TOKENS]
+                to[pl.ds(pl.multiple_of(k_row(2 * i + n), RANKS), RANKS), :] = k[:, n * TOKENS : (n + 1) * TOKENS]
             return carry
 
         lax.fori_loop(0, count // 2, body, 0)
@@ -114,14 +115,32 @@
     loads[1].wait()
     loads[2].wait()
     loads[3].wait()
-    project(QUERIES, xq, gq, pq)
+
+
+    def q_row(j, part):
+        share = QUERIES // CORES
+        return lax.div(j, share) * Q_HALF + part * Q_PART + lax.rem(j, share) * RANKS
+
+    project(QUERIES, xq, gq, pq, lambda j: q_row(j, 0), lambda j: q_row(j, 1))
+    loads[4].wait()
+    loads[5].wait()
+    project(DEMOS, xd, gd, pd, lambda j: j * PAIR + RANKS, lambda j: j * PAIR)
+    for n in (6, 7, 8, 9):
+        loads[n].wait()
+    mom[0:RANKS, :] = ADAM_ONE * md[...]
+    vel[0:RANKS, :] = ADAM_TWO * vd[...]
+    mom[RANKS:, :] = ADAM_ONE * mu[...]
+    vel[RANKS:, :] = ADAM_TWO * vu[...]
+
     pl.semaphore_wait(barrier, RINGS - 1 + 6)
 
     def to_core(n, src, dst):
         return pltpu.make_async_remote_copy(src, dst, core_send.at[n], core_recv.at[n], device_id=core_peer, device_id_type=MESH)
 
     q_cross = to_core(0, pq.at[pl.ds(pl.multiple_of(other * Q_HALF, Q_HALF), Q_HALF)], pq_in)
+    d_cross = to_core(1, pd.at[pl.ds(pl.multiple_of(other * D_HALF, D_HALF), D_HALF)], pd_in)
     q_cross.start()
+    d_cross.start()
 
     def fold(half, own, came, send, step):
         def body(i, carry):
@@ -133,12 +152,12 @@
 
         lax.fori_loop(0, half // step, body, 0)
 
-    def scatter(n, unit, send, slots):
+    def scatter(n, part):
         def body(i, carry):
             to = z_peer(far_first(i, RINGS))
             pltpu.make_async_remote_copy(
-                send.at[pl.ds(pl.multiple_of(to * unit, unit), unit)],
-                slots.at[z],
+                rq.at[pl.ds(pl.multiple_of(part * Q_PART + to * Q_UNIT, Q_UNIT), Q_UNIT)],
+                rq_in.at[part, z],
                 z_send.at[n],
                 z_recv.at[n],
                 device_id={"par": 2 * to + c},
@@ -167,61 +186,44 @@
 
     q_cross.wait()
     fold(Q_HALF, pq, pq_in, rq, 128)
-    scatter(0, Q_UNIT, rq, rq_in)
-    loads[4].wait()
-    loads[5].wait()
-    project(DEMOS, xd, gd, pd)
-    d_cross = to_core(1, pd.at[pl.ds(pl.multiple_of(other * D_HALF, D_HALF), D_HALF)], pd_in)
-    d_cross.start()
-    for n in (6, 7, 8, 9):
-        loads[n].wait()
-    mom[0:RANKS, :] = ADAM_ONE * md[...]
-    vel[0:RANKS, :] = ADAM_TWO * vd[...]
-    mom[RANKS:, :] = ADAM_ONE * mu[...]
-    vel[RANKS:, :] = ADAM_TWO * vu[...]
-
+    scatter(0, 0)
+    scatter(1, 1)
     d_cross.wait()
     fold(D_HALF, pd, pd_in, rd, 128)
     parity, place = lax.rem(z, 2), lax.div(z, 2)
     sides = (lax.rem(z + 1 - 2 * parity, RINGS), lax.rem(z + RINGS - 1 + 2 * parity, RINGS))
 
-    def to_sides(n, src, src_at, dst, dst_at):
+    def to_side(side, n, src, src_at, dst, dst_at):
         def body(m, carry):
-            for side, to in enumerate(sides):
-                at = pl.multiple_of(m * D_UNIT + side * D_SIDE, D_SIDE)
-                pltpu.make_async_remote_copy(
-                    src.at[pl.ds(src_at + at, D_SIDE)],
-                    dst.at[pl.ds(dst_at + at, D_SIDE)],
-                    z_send.at[n],
-                    z_recv.at[n],
-                    device_id={"par": 2 * to + c},
-                    device_id_type=MESH,
-                ).start()
+            at = pl.multiple_of(m * D_UNIT + side * D_SIDE, D_SIDE)
+            pltpu.make_async_remote_copy(
+                src.at[pl.ds(src_at + at, D_SIDE)],
+                dst.at[pl.ds(dst_at + at, D_SIDE)],
+                z_send.at[n],
+                z_recv.at[n],
+                device_id={"par": 2 * sides[side] + c},
+                device_id_type=MESH,
+            ).start()
             return carry
 
         lax.fori_loop(0, CLASS, body, 0)
 
-    to_sides(2, rd, pl.multiple_of((1 - parity) * D_CLASS, D_CLASS), rd_in, 0)
-
-    def gather_sum(n, unit, own, slots):
-        await_bytes(slots.at[pl.ds(0, RINGS - 1)], z_recv.at[n])
-        total = own[pl.ds(pl.multiple_of(z * unit, unit), unit), :]
-
-        def body(k, total):
-            return total + slots[z_peer(k)].astype(F32)
-
-        return lax.fori_loop(1, RINGS, body, total)
-
+    for side in range(2):
+        to_side(side, 5, rd, pl.multiple_of((1 - parity) * D_CLASS, D_CLASS), rd_in, 0)
     def weigh(rows, length):
         position = iota((1, TOKENS), 1)
         weight = jnp.where(position < length, 1.0 / jnp.full((1, TOKENS), length, F32), 0.0)
         return (rows * weight).astype(BF16)
 
-    q_total = gather_sum(0, Q_UNIT, pq_in, rq_in)
-    q_at = pl.multiple_of(c * Q_HALF + z * Q_UNIT, Q_UNIT)
-    hq[pl.ds(q_at, Q_UNIT), :] = weigh(q_total, qlen[lax.div(c * RINGS + z, PAIR // Q_UNIT)])
-    spread(1, Q_UNIT, hq, q_at)
-    await_bytes(rd_in, z_recv.at[2])
+    q_length = qlen[lax.div(c * RINGS + z, RINGS * CORES // QUERIES)]
+    for part in range(2):
+        await_bytes(rq_in.at[part, pl.ds(0, RINGS - 1)], z_recv.at[part])
+        own = pq_in[pl.ds(pl.multiple_of(part * Q_PART + z * Q_UNIT, Q_UNIT), Q_UNIT), :]
+        q_total = lax.fori_loop(1, RINGS, lambda k, total, part=part: total + rq_in[part, z_peer(k)].astype(F32), own)
+        q_at = pl.multiple_of(c * Q_HALF + part * Q_PART + z * Q_UNIT, Q_UNIT)
+        hq[pl.ds(q_at, Q_UNIT), :] = weigh(q_total, q_length)
+        spread(2 + part, Q_UNIT, hq, q_at)
+    await_bytes(rd_in, z_recv.at[5])
 
     def fold_class(i, carry):
         at = pl.multiple_of(i * D_UNIT, D_UNIT)
@@ -236,34 +238,24 @@
     def class_peer(i):
         return lax.rem(place + far_first(i, CLASS), CLASS)
 
-    def to_class(i, carry):
-        m = class_peer(i)
-        pltpu.make_async_remote_copy(
-            re.at[pl.ds(pl.multiple_of(m * D_UNIT, D_UNIT), D_UNIT)],
-            re_in.at[place],
-            z_send.at[3],
-            z_recv.at[3],
-            device_id={"par": 2 * (2 * m + parity) + c},
-            device_id_type=MESH,
-        ).start()
-        return carry
-
-    lax.fori_loop(0, CLASS - 1, to_class, 0)
-
-    await_bytes(hq.at[pl.ds(0, (RINGS - 1) * Q_UNIT)], z_recv.at[1])
-    q_half = hq.at[pl.ds(pl.multiple_of(c * Q_HALF, Q_HALF), Q_HALF)]
-    q_share = to_core(2, q_half, q_half)
-    q_share.start()
-    q_share.wait()
-
-    for j in range(QUERIES):
-        tokens = pl.ds(j * TOKENS, TOKENS)
-        down_grad = nn(hq[pl.ds(j * PAIR + RANKS, RANKS), :], xq[tokens, :])
-        up_grad = nn(hq[pl.ds(j * PAIR, RANKS), :], gq[tokens, :])
-        for h in range(2):
-            lanes = slice(h * LANES, (h + 1) * LANES)
-            qs[h, pl.ds(j, RANKS, stride=QUERIES), :] = down_grad[:, lanes]
-            qs[h, pl.ds(RANKS * QUERIES + j, RANKS, stride=QUERIES), :] = up_grad[:, lanes]
+    def class_sums(side):
+        def body(i, carry):
+            m = class_peer(i)
+            pltpu.make_async_remote_copy(
+                re.at[pl.ds(pl.multiple_of(m * D_UNIT + side * D_SIDE, D_SIDE), D_SIDE)],
+                re_in.at[side, place],
+                z_send.at[6 + side],
+                z_recv.at[6 + side],
+                device_id={"par": 2 * (2 * m + parity) + c},
+                device_id_type=MESH,
+            ).start()
+            return carry
+
+        lax.fori_loop(0, CLASS - 1, body, 0)
+
+    class_sums(0)
+    class_sums(1)
+
     piece_rows = RANKS * QUERIES
 
     def q_copy(block, piece, to):
@@ -271,29 +263,48 @@
             qall.at[block, piece], qall.at[block, piece], q_send.at[0], q_recv.at[block, piece], device_id=to, device_id_type=MESH
         )
 
-    for piece in range(4):
-        h, part = piece // 2, piece % 2
-        qall[e, piece] = qs[h, pl.ds(part * piece_rows, piece_rows), :].astype(BF16)
-        for to in (up, down, across):
-            q_copy(e, piece, to).start()
-
-    await_bytes(re_in.at[pl.ds(0, CLASS - 1)], z_recv.at[3])
-    d_place = pl.multiple_of(parity * D_CLASS + place * D_UNIT, D_UNIT)
-    d_total = lax.fori_loop(
-        1, CLASS, lambda k, total: total + re_in[lax.rem(place + k, CLASS)].astype(F32), pd_in[pl.ds(d_place, D_UNIT), :]
-    )
-    d_at = pl.multiple_of(c * D_HALF + d_place, D_UNIT)
-    for k in range(D_UNIT // GRAIN):
-        demo = lax.div(lax.div(d_at, GRAIN) + k, PAIR // GRAIN)
-        hd[pl.ds(d_at + k * GRAIN, GRAIN), :] = weigh(d_total[k * GRAIN : (k + 1) * GRAIN], dlen[demo])
-
-    def spread_class(i, carry):
-        ref = hd.at[pl.ds(d_at, D_UNIT)]
-        to = {"par": 2 * (2 * class_peer(i) + parity) + c}
-        pltpu.make_async_remote_copy(ref, ref, z_send.at[5], z_recv.at[5], device_id=to, device_id_type=MESH).start()
-        return carry
-
-    lax.fori_loop(0, CLASS - 1, spread_class, 0)
+    for part, array in ((0, xq), (1, gq)):
+        await_bytes(hq.at[pl.ds(0, (RINGS - 1) * Q_UNIT)], z_recv.at[2 + part])
+        own = hq.at[pl.ds(pl.multiple_of(c * Q_HALF + part * Q_PART, Q_PART), Q_PART)]
+        q_share = to_core(2 + part, own, own)
+        q_share.start()
+        q_share.wait()
+        for j in range(QUERIES):
+            at = (j // 4) * Q_HALF + part * Q_PART + (j % 4) * RANKS
+            grad = nn(hq[pl.ds(at, RANKS), :], array[pl.ds(j * TOKENS, TOKENS), :])
+            for h in range(2):
+                qs[h, pl.ds(part * piece_rows + j, RANKS, stride=QUERIES), :] = grad[:, h * LANES : (h + 1) * LANES]
+        for h in range(2):
+            qall[e, 2 * part + h] = qs[h, pl.ds(part * piece_rows, piece_rows), :].astype(BF16)
+            for to in (up, down, across):
+                q_copy(e, 2 * part + h, to).start()
+
+    d_class = pl.multiple_of(c * D_HALF + parity * D_CLASS, D_CLASS)
+
+    def weigh_side(side):
+        await_bytes(re_in.at[side, pl.ds(0, CLASS - 1)], z_recv.at[6 + side])
+        at = pl.multiple_of(parity * D_CLASS + place * D_UNIT + side * D_SIDE, D_SIDE)
+        total = lax.fori_loop(
+            1, CLASS, lambda k, total: total + re_in[side, lax.rem(place + k, CLASS)].astype(F32), pd_in[pl.ds(at, D_SIDE), :]
+        )
+        at = pl.multiple_of(c * D_HALF + at, D_SIDE)
+        for k in range(D_SIDE // GRAIN):
+            demo = lax.div(lax.div(at, GRAIN) + k, PAIR // GRAIN)
+            hd[pl.ds(at + k * GRAIN, GRAIN), :] = weigh(total[k * GRAIN : (k + 1) * GRAIN], dlen[demo])
+
+        def spread_class(i, carry):
+            ref = hd.at[pl.ds(at, D_SIDE)]
+            to = {"par": 2 * (2 * class_peer(i) + parity) + c}
+            pltpu.make_async_remote_copy(ref, ref, z_send.at[8 + side], z_recv.at[8 + side], device_id=to, device_id_type=MESH).start()
+            return carry
+
+        lax.fori_loop(0, CLASS - 1, spread_class, 0)
+
+    def pass_side(side):
+        await_bytes(hd.at[pl.ds(0, (CLASS - 1) * D_SIDE)], z_recv.at[8 + side])
+        to_side(side, 10 + side, hd, d_class, hd, d_class)
+
+    weigh_side(0)
 
     above = 2 * lax.rem(y + 1, ROWS) + x
     below = 2 * lax.rem(y + ROWS - 1, ROWS) + x
@@ -307,6 +318,8 @@
         await_bytes(qall.at[block, piece], q_recv.at[block, piece])
 
     for piece in range(4):
+        if piece == 1:
+            weigh_side(1)
         for block in (side, above, below):
             arrived(block, piece)
         if piece < 2:
@@ -317,18 +330,8 @@
             q_copy(below, piece, up).start()
             q_copy(above, piece, across).start()
             q_copy(below, piece, across).start()
-    await_bytes(hd.at[pl.ds(0, (CLASS - 1) * D_UNIT)], z_recv.at[5])
-    d_class = pl.multiple_of(c * D_HALF + parity * D_CLASS, D_CLASS)
-    to_sides(6, hd, d_class, hd, d_class)
-    arrived(beyond, 0)
-    q_copy(beyond, 0, across).start()
-    arrived(side_above, 1)
-    q_copy(side_above, 1, down).start()
-    arrived(side_below, 3)
-    q_copy(side_below, 3, up).start()
-    arrived(beyond, 2)
-    q_copy(beyond, 2, across).start()
-
+    pass_side(0)
+    pass_side(1)
     norms[...] = jnp.zeros_like(norms)
 
     def query_norms(n, carry):
@@ -341,9 +344,10 @@
 
     for block in (e, side, above, below):
         query_norms(block, 0)
-    await_bytes(hd.at[pl.ds(0, D_CLASS)], z_recv.at[6])
+    for side in range(2):
+        await_bytes(hd.at[pl.ds(0, CLASS * D_SIDE)], z_recv.at[10 + side])
     d_half = hd.at[pl.ds(pl.multiple_of(c * D_HALF, D_HALF), D_HALF)]
-    d_share = to_core(3, d_half, d_half)
+    d_share = to_core(4, d_half, d_half)
     d_share.start()
 
 
@@ -366,6 +370,15 @@
 
     first = c * (DEMOS // CORES)
     lax.fori_loop(first, first + DEMOS // CORES, update, 0)
+    arrived(beyond, 0)
+    q_copy(beyond, 0, across).start()
+    arrived(side_above, 1)
+    q_copy(side_above, 1, down).start()
+    arrived(side_below, 3)
+    q_copy(side_below, 3, up).start()
+    arrived(beyond, 2)
+    q_copy(beyond, 2, across).start()
+
     d_share.wait()
     first = other * (DEMOS // CORES)
     lax.fori_loop(first, first + DEMOS // CORES, update, 0)
@@ -384,7 +397,7 @@
                 left = jnp.concatenate([us[h, pl.ds(u_at, 2 * DEMOS), :] for h in range(2)], axis=1).astype(BF16)
                 right = jnp.concatenate(
                     [
-                        jnp.concatenate([qall[n, 2 * h + part, pl.ds(q_at, 2 * QUERIES), :] for n in range(EX)], axis=0)
+                        jnp.concatenate([qall[n, 2 * part + h, pl.ds(q_at, 2 * QUERIES), :] for n in range(EX)], axis=0)
                         for h in range(2)
                     ],
                     axis=1,
@@ -408,14 +421,12 @@
     row = iota((8, LANES), 0)
 
     def packed(core):
-        chosen, at = iota((8, DEMOS), 0), iota((8, DEMOS), 1)
-        first = ((chosen + 12 * core) == at) & (chosen < 6)
-        last = ((chosen + 12 * core + 6) == at) & (chosen < 6)
-        body = jnp.where(left_lanes, nn(first.astype(F32), twice, EXACT), nn(last.astype(F32), twice, EXACT))
+        left, right = jnp.where(core == 0, twice[0:6], twice[12:18]), jnp.where(core == 0, twice[6:12], twice[18:24])
+        body = jnp.concatenate([jnp.where(left_lanes[0:6], left, right), jnp.zeros((2, LANES), F32)], axis=0)
         return jnp.where(row == 6, sums, body)
 
     fin_out[...] = packed(other)
-    cross = to_core(4, fin_out, fin_in)
+    cross = to_core(5, fin_out, fin_in)
     cross.start()
     mine = packed(c)
     cross.wait()
@@ -452,18 +463,16 @@
         copy.wait()
     fin_part[c] = fin_mine[...] + fin_ends[0]
     fin_part[other] = fin_ends[1] + fin_ends[2]
-    both = jnp.concatenate([fin_part[0], fin_part[1]], axis=0)
-    demo, at = iota((DEMOS, 16), 0), iota((DEMOS, 16), 1)
-    rows = nn((at == 8 * lax.div(demo, 12) + lax.rem(demo, 6)).astype(F32), both, EXACT)
-    late = lax.rem(lax.div(iota((DEMOS, LANES // 2), 0), 6), 2) == 1
-    out[...] = jnp.where(late, rows[:, LANES // 2 :], rows[:, : LANES // 2])
-
-    await_bytes(rq.at[pl.ds(0, (RINGS - 1) * Q_UNIT)], z_send.at[0])
-    await_bytes(hq.at[pl.ds(0, (RINGS - 1) * Q_UNIT)], z_send.at[1])
-    await_bytes(rd.at[pl.ds(0, D_CLASS)], z_send.at[2])
-    await_bytes(re_in.at[pl.ds(0, CLASS - 1)], z_send.at[3])
-    await_bytes(hd.at[pl.ds(0, (CLASS - 1) * D_UNIT)], z_send.at[5])
-    await_bytes(hd.at[pl.ds(0, D_CLASS)], z_send.at[6])
+    rows = [fin_part[n][0:6, h * (LANES // 2) : (h + 1) * (LANES // 2)] for n in range(2) for h in range(2)]
+    out[...] = jnp.concatenate(rows, axis=0)
+
+    for n in range(4):
+        await_bytes(rq.at[pl.ds(0, (RINGS - 1) * Q_UNIT)], z_send.at[n])
+    await_bytes(rd.at[pl.ds(0, D_CLASS)], z_send.at[5])
+    for side in range(2):
+        await_bytes(re_in.at[side, pl.ds(0, CLASS - 1)], z_send.at[6 + side])
+        await_bytes(hd.at[pl.ds(0, (CLASS - 1) * D_SIDE)], z_send.at[8 + side])
+        await_bytes(hd.at[pl.ds(0, CLASS * D_SIDE)], z_send.at[10 + side])
     await_bytes(fin_slots.at[pl.ds(0, RINGS - 1)], z_send.at[4])
     await_bytes(qall.at[pl.ds(0, EX - 1)], q_send.at[0])
 
@@ -509,11 +518,11 @@
             vmem((DEMOS * PAIR, TOKENS), F32),
             vmem((D_HALF, TOKENS), F32),
             vmem((Q_HALF, TOKENS), BF16),
-            vmem((RINGS, Q_UNIT, TOKENS), BF16),
+            vmem((2, RINGS, Q_UNIT, TOKENS), BF16),
             vmem((D_HALF, TOKENS), BF16),
             vmem((D_CLASS, TOKENS), BF16),
             vmem((D_CLASS, TOKENS), BF16),
-            vmem((CLASS, D_UNIT, TOKENS), BF16),
+            vmem((2, CLASS, D_SIDE, TOKENS), BF16),
             vmem((QUERIES * PAIR, TOKENS), BF16),
             vmem((DEMOS * PAIR, TOKENS), BF16),
             vmem((2, PAIR * QUERIES, LANES), F32),
@@ -527,10 +536,10 @@
             vmem((2, 8, LANES), F32),
             vmem((3, 8, LANES), F32),
             dma((10,)),
-            dma((5,)),
-            dma((5,)),
-            dma((7,)),
-            dma((7,)),
+            dma((6,)),
+            dma((6,)),
+            dma((12,)),
+            dma((12,)),
             dma((1,)),
             dma((EX, 4)),
             dma((3,)),

time: 91.9 us -> 85.1 us (0.926)
  Pallas kernels: 89.8 us -> 82.9 us
    pallas_call x1, Pallas kernels: 89.8 us -> 82.9 us  [shards(): pl.pallas_call(kernel, out_shape=jax.ShapeDtypeStruct((DEMOS, EX * QUERIE...]
where the time goes in v3:
time: 85.1 us; the launch traced here: 84.9 us
  Pallas kernels  82.9 us (97%)
  local copies, waits for them, and re-layouts  1.31 us (2%)
    pallas_call x1, Pallas kernels, shards(): pl.pallas_call(kernel, out_shape=jax.ShapeDtypeStruct((DEMOS, EX * QUERIE...  82.9 us

profile of v3, /device:TPU:1, one launch (start us, length us, event | category | flops | bytes accessed | tf_op | source)
XLA Modules:
  0.0 84.9 jit_solution(14472147148108794620)
XLA Ops:
  0.7 82.9 %shard_map.127 = f32[24,64]{1,0:T(8,128)} custom-call(bf16[1024,256]{1,0:T(8,128)(2,1)} %bitcast.18, bf16[1024,256]{1,0:T(8,128)(2,1)} %bitcast.19, bf16[3072,256]{1,0:T(8,128)(2,1)} %bitcast.16, bf16[3072,256]{1,0:T(8,128)(2,1)} %bitcast.17, bf16[64,256]{1,0:T(8,128)(2,1)} %bitcast.24, bf16[64,256]{1,0:T(8,128)(2,1)} %bitcast.25, f32[64,256]{1,0:T(8,128)} %bitcast.20, ...), custom_call_target="tpu_custom_call" | custom-call | tf_op jit(solution)/shard_map/pallas_call | solution.py:498
  83.6 1.3 %copy.16 = f32[24,64]{1,0:T(8,128)} copy(f32[24,64]{1,0:T(8,128)} %shard_map.127) | data formatting | bytes 12288

commit v4 on v3

--- a/solution.py
+++ b/solution.py
@@ -57,9 +57,9 @@
     pq, pq_in, pd, pd_in,
     rq, rq_in, rd, rd_in, re, re_in,
     hq, hd,
-    qs, us, qall, norms,
+    qs, us, qall, norms, near_x, near_k,
     fin_out, fin_in, fin_mine, fin_slots, fin_part, fin_ends,
-    load_sem, core_send, core_recv, z_send, z_recv, q_send, q_recv, end_send, end_recv,
+    load_sem, core_send, core_recv, z_send, z_recv, q_send, q_recv, near_send, near_recv, end_send, end_recv,
 ):
     me = lax.axis_index("par")
     z, c = lax.div(me, CORES), lax.rem(me, CORES)
@@ -138,19 +138,36 @@
         return pltpu.make_async_remote_copy(src, dst, core_send.at[n], core_recv.at[n], device_id=core_peer, device_id_type=MESH)
 
     q_cross = to_core(0, pq.at[pl.ds(pl.multiple_of(other * Q_HALF, Q_HALF), Q_HALF)], pq_in)
-    d_cross = to_core(1, pd.at[pl.ds(pl.multiple_of(other * D_HALF, D_HALF), D_HALF)], pd_in)
+    parity, place = lax.rem(z, 2), lax.div(z, 2)
+    leaves, stays = pl.multiple_of((1 - parity) * D_CLASS, D_CLASS), pl.multiple_of(parity * D_CLASS, D_CLASS)
+    d_cross = [
+        to_core(n, pd.at[pl.ds(pl.multiple_of(other * D_HALF + at, D_CLASS), D_CLASS)], pd_in.at[pl.ds(at, D_CLASS)])
+        for n, at in ((1, leaves), (6, stays))
+    ]
     q_cross.start()
-    d_cross.start()
-
-    def fold(half, own, came, send, step):
+
+    near = ((0, across), (2, up), (1, down))
+
+    def near_copy(n, src, dst, slot, to):
+        return pltpu.make_async_remote_copy(src, dst, near_send.at[n, slot], near_recv.at[n, slot], device_id=to, device_id_type=MESH)
+
+    x_copies = [near_copy(0, xq, near_x.at[slot], slot, to) for slot, to in near]
+    for copy in x_copies:
+        copy.start()
+    d_cross[0].start()
+    d_cross[1].start()
+
+    def fold(count, own, own_at, came, came_at, send, send_at, step):
         def body(i, carry):
             at = pl.multiple_of(i * step, step)
-            total = own[pl.ds(pl.multiple_of(c * half + at, step), step), :] + came[pl.ds(at, step), :]
-            came[pl.ds(at, step), :] = total
-            send[pl.ds(at, step), :] = total.astype(BF16)
+            rows = pl.ds(pl.multiple_of(came_at + at, step), step)
+            total = own[pl.ds(pl.multiple_of(own_at + at, step), step), :] + came[rows, :]
+            came[rows, :] = total
+            if send is not None:
+                send[pl.ds(pl.multiple_of(send_at + at, step), step), :] = total.astype(BF16)
             return carry
 
-        lax.fori_loop(0, half // step, body, 0)
+        lax.fori_loop(0, count // step, body, 0)
 
     def scatter(n, part):
         def body(i, carry):
@@ -185,12 +202,11 @@
         pltpu.make_async_copy(ref, ref, sem).wait()
 
     q_cross.wait()
-    fold(Q_HALF, pq, pq_in, rq, 128)
+    fold(Q_HALF, pq, c * Q_HALF, pq_in, 0, rq, 0, 128)
     scatter(0, 0)
     scatter(1, 1)
-    d_cross.wait()
-    fold(D_HALF, pd, pd_in, rd, 128)
-    parity, place = lax.rem(z, 2), lax.div(z, 2)
+    d_cross[0].wait()
+    fold(D_CLASS, pd, c * D_HALF + leaves, pd_in, leaves, rd, 0, 128)
     sides = (lax.rem(z + 1 - 2 * parity, RINGS), lax.rem(z + RINGS - 1 + 2 * parity, RINGS))
 
     def to_side(side, n, src, src_at, dst, dst_at):
@@ -209,21 +225,13 @@
         lax.fori_loop(0, CLASS, body, 0)
 
     for side in range(2):
-        to_side(side, 5, rd, pl.multiple_of((1 - parity) * D_CLASS, D_CLASS), rd_in, 0)
+        to_side(side, 5, rd, 0, rd_in, 0)
+    d_cross[1].wait()
+    fold(D_CLASS, pd, c * D_HALF + stays, pd_in, stays, None, 0, 128)
     def weigh(rows, length):
         position = iota((1, TOKENS), 1)
         weight = jnp.where(position < length, 1.0 / jnp.full((1, TOKENS), length, F32), 0.0)
         return (rows * weight).astype(BF16)
-
-    q_length = qlen[lax.div(c * RINGS + z, RINGS * CORES // QUERIES)]
-    for part in range(2):
-        await_bytes(rq_in.at[part, pl.ds(0, RINGS - 1)], z_recv.at[part])
-        own = pq_in[pl.ds(pl.multiple_of(part * Q_PART + z * Q_UNIT, Q_UNIT), Q_UNIT), :]
-        q_total = lax.fori_loop(1, RINGS, lambda k, total, part=part: total + rq_in[part, z_peer(k)].astype(F32), own)
-        q_at = pl.multiple_of(c * Q_HALF + part * Q_PART + z * Q_UNIT, Q_UNIT)
-        hq[pl.ds(q_at, Q_UNIT), :] = weigh(q_total, q_length)
-        spread(2 + part, Q_UNIT, hq, q_at)
-    await_bytes(rd_in, z_recv.at[5])
 
     def fold_class(i, carry):
         at = pl.multiple_of(i * D_UNIT, D_UNIT)
@@ -232,8 +240,6 @@
         pd_in[own, :] = total
         re[pl.ds(at, D_UNIT), :] = total.astype(BF16)
         return carry
-
-    lax.fori_loop(0, CLASS, fold_class, 0)
 
     def class_peer(i):
         return lax.rem(place + far_first(i, CLASS), CLASS)
@@ -253,32 +259,64 @@
 
         lax.fori_loop(0, CLASS - 1, body, 0)
 
+    q_length = qlen[lax.div(c * RINGS + z, RINGS * CORES // QUERIES)]
+    for part in range(2):
+        await_bytes(rq_in.at[part, pl.ds(0, RINGS - 1)], z_recv.at[part])
+        own = pq_in[pl.ds(pl.multiple_of(part * Q_PART + z * Q_UNIT, Q_UNIT), Q_UNIT), :]
+        q_total = lax.fori_loop(1, RINGS, lambda k, total, part=part: total + rq_in[part, z_peer(k)].astype(F32), own)
+        q_at = pl.multiple_of(c * Q_HALF + part * Q_PART + z * Q_UNIT, Q_UNIT)
+        hq[pl.ds(q_at, Q_UNIT), :] = weigh(q_total, q_length)
+        spread(2 + part, Q_UNIT, hq, q_at)
+    await_bytes(rd_in, z_recv.at[5])
+    lax.fori_loop(0, CLASS, fold_class, 0)
     class_sums(0)
     class_sums(1)
-
     piece_rows = RANKS * QUERIES
 
-    def q_copy(block, piece, to):
+    def q_copy(block, piece, to, n=0):
         return pltpu.make_async_remote_copy(
-            qall.at[block, piece], qall.at[block, piece], q_send.at[0], q_recv.at[block, piece], device_id=to, device_id_type=MESH
+            qall.at[block, piece], qall.at[block, piece], q_send.at[n], q_recv.at[block, piece], device_id=to, device_id_type=MESH
         )
 
+    def gradients(block, part, rows, array):
+        for j in range(QUERIES):
+            grad = nn(rows(j), array(j))
+            for h in range(2):
+                qs[h, pl.ds(part * piece_rows + j, RANKS, stride=QUERIES), :] = grad[:, h * LANES : (h + 1) * LANES]
+        for h in range(2):
+            qall[block, 2 * part + h] = qs[h, pl.ds(part * piece_rows, piece_rows), :].astype(BF16)
+
+    k_copies = []
     for part, array in ((0, xq), (1, gq)):
         await_bytes(hq.at[pl.ds(0, (RINGS - 1) * Q_UNIT)], z_recv.at[2 + part])
         own = hq.at[pl.ds(pl.multiple_of(c * Q_HALF + part * Q_PART, Q_PART), Q_PART)]
         q_share = to_core(2 + part, own, own)
         q_share.start()
         q_share.wait()
-        for j in range(QUERIES):
-            at = (j // 4) * Q_HALF + part * Q_PART + (j % 4) * RANKS
-            grad = nn(hq[pl.ds(at, RANKS), :], array[pl.ds(j * TOKENS, TOKENS), :])
+        if part == 0:
+            for n in range(CORES):
+                for slot, to in near:
+                    copy = near_copy(1 + n, hq.at[pl.ds(n * Q_HALF, Q_PART)], near_k.at[slot, pl.ds(n * Q_PART, Q_PART)], slot, to)
+                    copy.start()
+                    k_copies.append(copy)
+        gradients(
+            e,
+            part,
+            lambda j, part=part: hq[pl.ds((j // 4) * Q_HALF + part * Q_PART + (j % 4) * RANKS, RANKS), :],
+            lambda j, array=array: array[pl.ds(j * TOKENS, TOKENS), :],
+        )
+        if part == 1:
             for h in range(2):
-                qs[h, pl.ds(part * piece_rows + j, RANKS, stride=QUERIES), :] = grad[:, h * LANES : (h + 1) * LANES]
-        for h in range(2):
-            qall[e, 2 * part + h] = qs[h, pl.ds(part * piece_rows, piece_rows), :].astype(BF16)
-            for to in (up, down, across):
-                q_copy(e, 2 * part + h, to).start()
-
+                for to in (up, down, across):
+                    q_copy(e, 2 + h, to).start()
+
+    above = 2 * lax.rem(y + 1, ROWS) + x
+    below = 2 * lax.rem(y + ROWS - 1, ROWS) + x
+    beyond = 2 * lax.rem(y + 2, ROWS) + x
+    side = 2 * y + 1 - x
+    side_above = 2 * lax.rem(y + 1, ROWS) + 1 - x
+    side_below = 2 * lax.rem(y + ROWS - 1, ROWS) + 1 - x
+    side_beyond = 2 * lax.rem(y + 2, ROWS) + 1 - x
     d_class = pl.multiple_of(c * D_HALF + parity * D_CLASS, D_CLASS)
 
     def weigh_side(side):
@@ -305,31 +343,40 @@
         to_side(side, 10 + side, hd, d_class, hd, d_class)
 
     weigh_side(0)
-
-    above = 2 * lax.rem(y + 1, ROWS) + x
-    below = 2 * lax.rem(y + ROWS - 1, ROWS) + x
-    beyond = 2 * lax.rem(y + 2, ROWS) + x
-    side = 2 * y + 1 - x
-    side_above = 2 * lax.rem(y + 1, ROWS) + 1 - x
-    side_below = 2 * lax.rem(y + ROWS - 1, ROWS) + 1 - x
-    side_beyond = 2 * lax.rem(y + 2, ROWS) + 1 - x
+    weigh_side(1)
+    for copy in x_copies + k_copies:
+        copy.wait()
+    for slot, block in ((1, above), (2, below), (0, side)):
+        gradients(
+            block,
+            0,
+            lambda j, slot=slot: near_k[slot, pl.ds(j * RANKS, RANKS), :],
+            lambda j, slot=slot: near_x[slot, pl.ds(j * TOKENS, TOKENS), :],
+        )
+        if slot == 1:
+            q_copy(above, 0, down).start()
+            q_copy(above, 0, across).start()
+        elif slot == 2:
+            q_copy(below, 1, up).start()
+            q_copy(below, 0, across).start()
+        else:
+            q_copy(side, 1, down).start()
+            q_copy(side, 1, up).start()
 
     def arrived(block, piece):
         await_bytes(qall.at[block, piece], q_recv.at[block, piece])
 
-    for piece in range(4):
-        if piece == 1:
-            weigh_side(1)
+    for piece in (2, 3):
         for block in (side, above, below):
             arrived(block, piece)
-        if piece < 2:
-            q_copy(above, piece, down).start()
-            q_copy(side, piece, up).start()
-            q_copy(side, piece, down).start()
+        if piece == 2:
+            q_copy(above, 2, down, 1).start()
+            q_copy(side, 2, down, 1).start()
+            q_copy(side, 2, up, 1).start()
         else:
-            q_copy(below, piece, up).start()
-            q_copy(above, piece, across).start()
-            q_copy(below, piece, across).start()
+            q_copy(below, 3, up, 1).start()
+            q_copy(above, 3, across, 1).start()
+            q_copy(below, 3, across, 1).start()
     pass_side(0)
     pass_side(1)
     norms[...] = jnp.zeros_like(norms)
@@ -344,12 +391,6 @@
 
     for block in (e, side, above, below):
         query_norms(block, 0)
-    for side in range(2):
-        await_bytes(hd.at[pl.ds(0, CLASS * D_SIDE)], z_recv.at[10 + side])
-    d_half = hd.at[pl.ds(pl.multiple_of(c * D_HALF, D_HALF), D_HALF)]
-    d_share = to_core(4, d_half, d_half)
-    d_share.start()
-
 
     def update(i, carry):
         tokens = pl.ds(pl.multiple_of(i * TOKENS, TOKENS), TOKENS)
@@ -368,22 +409,37 @@
         norms[pl.ds(EX * QUERIES + i, 1), :] = jnp.sum(squares, axis=0, keepdims=True)
         return carry
 
-    first = c * (DEMOS // CORES)
-    lax.fori_loop(first, first + DEMOS // CORES, update, 0)
-    arrived(beyond, 0)
-    q_copy(beyond, 0, across).start()
-    arrived(side_above, 1)
-    q_copy(side_above, 1, down).start()
-    arrived(side_below, 3)
-    q_copy(side_below, 3, up).start()
+    group = DEMOS // CORES // 2
+
+    def update_group(core, which):
+        first = core * (DEMOS // CORES) + which * group
+        lax.fori_loop(first, first + group, update, 0)
+
+    def share_class(n, which):
+        ref = hd.at[pl.ds(pl.multiple_of(c * D_HALF + which * D_CLASS, D_CLASS), D_CLASS)]
+        return to_core(n, ref, ref)
+
+    share = share_class(4, parity)
+    share.start()
+    update_group(c, parity)
+    share.wait()
+    update_group(other, parity)
+    arrived(side_above, 0)
+    q_copy(side_above, 0, down, 1).start()
+    arrived(side_below, 1)
+    q_copy(side_below, 1, up, 1).start()
     arrived(beyond, 2)
-    q_copy(beyond, 2, across).start()
-
-    d_share.wait()
-    first = other * (DEMOS // CORES)
-    lax.fori_loop(first, first + DEMOS // CORES, update, 0)
-
-    for block, pieces in ((beyond, (1, 3)), (side_above, (0, 2, 3)), (side_below, (0, 1, 2)), (side_beyond, (0, 1, 2, 3))):
+    q_copy(beyond, 2, across, 1).start()
+    arrived(beyond, 3)
+    q_copy(beyond, 3, across, 1).start()
+    for side in range(2):
+        await_bytes(hd.at[pl.ds(0, CLASS * D_SIDE)], z_recv.at[10 + side])
+    share = share_class(7, 1 - parity)
+    share.start()
+    update_group(c, 1 - parity)
+    share.wait()
+    update_group(other, 1 - parity)
+    for block, pieces in ((beyond, (0, 1)), (side_above, (1, 2, 3)), (side_below, (0, 2, 3)), (side_beyond, (0, 1, 2, 3))):
         for piece in pieces:
             arrived(block, piece)
         query_norms(block, 0)
@@ -474,7 +530,8 @@
         await_bytes(hd.at[pl.ds(0, (CLASS - 1) * D_SIDE)], z_send.at[8 + side])
         await_bytes(hd.at[pl.ds(0, CLASS * D_SIDE)], z_send.at[10 + side])
     await_bytes(fin_slots.at[pl.ds(0, RINGS - 1)], z_send.at[4])
-    await_bytes(qall.at[pl.ds(0, EX - 1)], q_send.at[0])
+    await_bytes(qall.at[pl.ds(0, 3)], q_send.at[0])
+    await_bytes(xd.at[pl.ds(0, 10 * piece_rows // 2)], q_send.at[1])
 
 
 def shards(
@@ -519,7 +576,7 @@
             vmem((D_HALF, TOKENS), F32),
             vmem((Q_HALF, TOKENS), BF16),
             vmem((2, RINGS, Q_UNIT, TOKENS), BF16),
-            vmem((D_HALF, TOKENS), BF16),
+            vmem((D_CLASS, TOKENS), BF16),
             vmem((D_CLASS, TOKENS), BF16),
             vmem((D_CLASS, TOKENS), BF16),
             vmem((2, CLASS, D_SIDE, TOKENS), BF16),
@@ -529,6 +586,8 @@
             vmem((2, PAIR * DEMOS, LANES), F32),
             vmem((EX, 4, RANKS * QUERIES, LANES), BF16),
             vmem((LANES, LANES), F32),
+            vmem((3, QUERIES * TOKENS, FEATURES), BF16),
+            vmem((3, QUERIES * RANKS, TOKENS), BF16),
             vmem((8, LANES), F32),
             vmem((8, LANES), F32),
             vmem((8, LANES), F32),
@@ -536,12 +595,14 @@
             vmem((2, 8, LANES), F32),
             vmem((3, 8, LANES), F32),
             dma((10,)),
-            dma((6,)),
-            dma((6,)),
+            dma((8,)),
+            dma((8,)),
             dma((12,)),
             dma((12,)),
-            dma((1,)),
+            dma((2,)),
             dma((EX, 4)),
+            dma((3, 3)),
+            dma((3, 3)),
             dma((3,)),
             dma((3,)),
         ],

time: 85.1 us -> 83.2 us (0.978)
  Pallas kernels: 82.9 us -> 80.7 us
    pallas_call x1, Pallas kernels: 82.9 us -> 80.7 us  [shards(): pl.pallas_call(kernel, out_shape=jax.ShapeDtypeStruct((DEMOS, EX * QUERIE...]
where the time goes in v4:
time: 83.2 us; the launch traced here: 82.7 us
  Pallas kernels  80.7 us (97%)
  local copies, waits for them, and re-layouts  1.31 us (2%)
    pallas_call x1, Pallas kernels, shards(): pl.pallas_call(kernel, out_shape=jax.ShapeDtypeStruct((DEMOS, EX * QUERIE...  80.7 us

profile of v4, /device:TPU:1, one launch (start us, length us, event | category | flops | bytes accessed | tf_op | source)
XLA Modules:
  0.0 82.7 jit_solution(5300242494139940205)
XLA Ops:
  0.7 80.7 %shard_map.127 = f32[24,64]{1,0:T(8,128)} custom-call(bf16[1024,256]{1,0:T(8,128)(2,1)} %bitcast.18, bf16[1024,256]{1,0:T(8,128)(2,1)} %bitcast.19, bf16[3072,256]{1,0:T(8,128)(2,1)} %bitcast.16, bf16[3072,256]{1,0:T(8,128)(2,1)} %bitcast.17, bf16[64,256]{1,0:T(8,128)(2,1)} %bitcast.24, bf16[64,256]{1,0:T(8,128)(2,1)} %bitcast.25, f32[64,256]{1,0:T(8,128)} %bitcast.20, ...), custom_call_target="tpu_custom_call" | custom-call | tf_op jit(solution)/shard_map/pallas_call | solution.py:555
  81.4 1.3 %copy.16 = f32[24,64]{1,0:T(8,128)} copy(f32[24,64]{1,0:T(8,128)} %shard_map.127) | data formatting | bytes 12288
